TPU v7x, 32 devices: a whole 2x2x4 slice. The times are simulated.
32 devices in a mesh: row: 4 (over x, core), col: 8 (over z, y).
Axes of the slice: x: 2, y: 2, z: 4, core: 2. Of those that a mesh axis runs over, the one named last changes fastest.
Arguments:
- object_field: float32 [2, 2048, 4096], P(None, 'row', 'col'), may hold values from -5 to 5
- probe: float32 [2, 256, 256], replicated, may hold values from -5 to 5
- amplitude: float32 [4, 8, 8, 256, 256], P('row', 'col'), may hold values from 0.2 to 3
- offsets: int32 [4, 8, 8, 2], P('row', 'col'), may hold values from 0 to 511
Outputs:
- object_grad: float32 [2, 2048, 4096], P(None, 'row', 'col')
- probe_grad: float32 [2, 256, 256], replicated
All inputs are finite; a program needn't handle non-finite values.
Results may differ from a plain program's by a relative error of at most 0.0003.
Values sent between devices are 32-bit elements; how exact they have to be, the bound alone decides.
A program may use at most 64 MiB of HBM per device.

v0:
```python
import math

import jax
import jax.numpy as jnp
from jax import lax
from jax.sharding import PartitionSpec as P


def passed_along(value, axis, steps):
    count = lax.axis_size(axis)
    first, last = (max(0, -steps), min(count, count - steps))
    return lax.ppermute(value, axis, [(source, source + steps) for source in range(first, last)])


def tables(size):
    index = jnp.arange(size, dtype=jnp.int32)
    product = index[:, None] * index[None, :] % size
    angle = product.astype(jnp.float32) * (2.0 * math.pi / size)
    scale = 1.0 / math.sqrt(size)
    return (jnp.cos(angle) * scale, jnp.sin(angle) * scale)


def matmul(left, right):
    return jnp.dot(left, right, precision=lax.Precision.HIGHEST, preferred_element_type=jnp.float32)


def transform(real_part, imag_part, cosine, sine, sign):
    left_r = matmul(cosine, real_part) - sign * matmul(sine, imag_part)
    left_i = matmul(cosine, imag_part) + sign * matmul(sine, real_part)
    out_r = matmul(left_r, cosine) - sign * matmul(left_i, sine)
    out_i = matmul(left_i, cosine) + sign * matmul(left_r, sine)
    return (out_r, out_i)


def patch_terms(view, probe, amp, cosine, sine):
    probe_r, probe_i = (probe[0], probe[1])
    view_r, view_i = (view[0], view[1])
    wave_r = probe_r * view_r - probe_i * view_i
    wave_i = probe_r * view_i + probe_i * view_r
    far_r, far_i = transform(wave_r, wave_i, cosine, sine, -1.0)
    modulus = jnp.sqrt(far_r * far_r + far_i * far_i)
    keep = 1.0 - amp / jnp.maximum(modulus, 0.5)
    chi_r, chi_i = transform(far_r * keep, far_i * keep, cosine, sine, 1.0)
    obj_term = jnp.stack([probe_r * chi_r + probe_i * chi_i, probe_r * chi_i - probe_i * chi_r])
    probe_term = jnp.stack([view_r * chi_r + view_i * chi_i, view_r * chi_i - view_i * chi_r])
    return (obj_term, probe_term)


def shards(object_field, probe, amplitude, offsets):
    tile_rows = object_field.shape[1]
    tile_cols = object_field.shape[2]
    side = probe.shape[1]
    positions = offsets.shape[2]
    cosine, sine = tables(side)
    below = passed_along(object_field[:, :side, :], "row", -1)
    tall = jnp.concatenate([object_field, below], axis=1)
    right = passed_along(tall[:, :, :side], "col", -1)
    extended = jnp.concatenate([tall, right], axis=2)

    def step(number, carry):
        grad, probe_acc = carry
        off = offsets[0, 0, number]
        top = off[0]
        left = off[1]
        zero = jnp.zeros((), jnp.int32)
        view = lax.dynamic_slice(extended, (zero, top, left), (2, side, side))
        obj_term, probe_term = patch_terms(view, probe, amplitude[0, 0, number], cosine, sine)
        old = lax.dynamic_slice(grad, (zero, top, left), (2, side, side))
        grad = lax.dynamic_update_slice(grad, old + obj_term, (zero, top, left))
        return (grad, probe_acc + probe_term)

    start = (jnp.zeros(extended.shape, jnp.float32), jnp.zeros((2, side, side), jnp.float32))
    grad, probe_acc = lax.fori_loop(0, positions, step, start)
    returned = passed_along(grad[:, :, tile_cols:], "col", 1)
    tall_grad = grad[:, :, :tile_cols].at[:, :, :side].add(returned)
    returned_rows = passed_along(tall_grad[:, tile_rows:, :], "row", 1)
    object_grad = tall_grad[:, :tile_rows, :].at[:, :side, :].add(returned_rows)
    partial_total = lax.psum(probe_acc, "col")
    probe_total = lax.psum(partial_total, "row")
    count = positions * lax.axis_size("row") * lax.axis_size("col")
    return (object_grad, probe_total / count)


def solution(mesh):
    placed = (
        P(None, "row", "col"),
        P(),
        P("row", "col", None, None, None),
        P("row", "col", None, None),
    )
    return jax.shard_map(
        shards, mesh=mesh, in_specs=placed, out_specs=(P(None, "row", "col"), P()), check_vma=False
    )
```

profile of v0, /device:TPU:0, one launch (start us, length us, event | category | flops | bytes accessed | tf_op | source)
XLA Modules:
  0.0 536.7 jit_solution(9101638636517774362)
XLA Ops:
  10.1 3.1 collective-permute-done
  16.8 27.7 %collective-permute-done.1 = f32[2,768,256]{2,1,0:T(8,128)S(1)} collective-permute-done((f32[2,768,256]{2,1,0:T(8,128)}, f32[2,768,256]{2,1,0:T(8,128)S(1)}, u32[]{:S(2)}, u32[]{:S(2)}) %collective-permute-start.1) | collective-permute-done | bytes 1572896 | tf_op jit(solution)/shard_map/ppermute | solution.py:12
  44.5 4.4 pad_maximum_fusion
  51.4 316.5 %while.19 = (s32[]{:T(128)}, f32[2,768,768]{2,1,0:T(8,128)}, f32[2,256,256]{2,1,0:T(8,128)S(1)}, s32[1,1,8,2]{2,3,1,0:T(2,128)S(1)}, f32[2,256,256]{2,1,0:T(8,12...) while((s32[]{:T(128)}, f32[2,768,768]{2,1,0:T(8,128)}, ...), condition=%wide.region_1.2_spmd.clone.clone, body=%wide.region_0.1_spmd.clone.clone.sunk | while | flops 3240099840 | bytes 19136796 | solution.py:73
  67.3 2.5 fusion.184
  80.2 2.7 add_bitcast_fusion.2
  84.4 6.2 %dynamic_update_slice.10 = f32[2,768,768]{2,1,0:T(8,128)} dynamic-update-slice(f32[2,768,768]{2,1,0:T(8,128)} %get-tuple-element.397, f32[2,256,256]{2,1,0:T(8,128)S(1)} %get-tuple-element.383, s32[]{:T(128)} %constant.116.clone.1..sunk, s32[]{:T(128)S(6)} %select_n.137, s32[]{:T(128)S(6)} %select_n.138) | dynamic-update-slice | bytes 1048580 | tf_op jit(solution)/shard_map/while/body/eval_jaxpr/dynamic_update_slice | solution.py:69
  106.4 2.5 fusion.184
  119.3 2.7 add_bitcast_fusion.2
  123.5 6.1 %dynamic_update_slice.10 = f32[2,768,768]{2,1,0:T(8,128)} dynamic-update-slice(f32[2,768,768]{2,1,0:T(8,128)} %get-tuple-element.397, f32[2,256,256]{2,1,0:T(8,128)S(1)} %get-tuple-element.383, s32[]{:T(128)} %constant.116.clone.1..sunk, s32[]{:T(128)S(6)} %select_n.137, s32[]{:T(128)S(6)} %select_n.138) | dynamic-update-slice | bytes 1048580 | tf_op jit(solution)/shard_map/while/body/eval_jaxpr/dynamic_update_slice | solution.py:69
  158.4 2.7 add_bitcast_fusion.2
  162.6 6.6 %dynamic_update_slice.10 = f32[2,768,768]{2,1,0:T(8,128)} dynamic-update-slice(f32[2,768,768]{2,1,0:T(8,128)} %get-tuple-element.397, f32[2,256,256]{2,1,0:T(8,128)S(1)} %get-tuple-element.383, s32[]{:T(128)} %constant.116.clone.1..sunk, s32[]{:T(128)S(6)} %select_n.137, s32[]{:T(128)S(6)} %select_n.138) | dynamic-update-slice | bytes 1048580 | tf_op jit(solution)/shard_map/while/body/eval_jaxpr/dynamic_update_slice | solution.py:69
  185.1 2.5 fusion.184
  198.0 2.7 add_bitcast_fusion.2
  202.3 6.5 %dynamic_update_slice.10 = f32[2,768,768]{2,1,0:T(8,128)} dynamic-update-slice(f32[2,768,768]{2,1,0:T(8,128)} %get-tuple-element.397, f32[2,256,256]{2,1,0:T(8,128)S(1)} %get-tuple-element.383, s32[]{:T(128)} %constant.116.clone.1..sunk, s32[]{:T(128)S(6)} %select_n.137, s32[]{:T(128)S(6)} %select_n.138) | dynamic-update-slice | bytes 1048580 | tf_op jit(solution)/shard_map/while/body/eval_jaxpr/dynamic_update_slice | solution.py:69
  224.7 2.5 fusion.184
  237.6 2.7 add_bitcast_fusion.2
  241.8 6.8 %dynamic_update_slice.10 = f32[2,768,768]{2,1,0:T(8,128)} dynamic-update-slice(f32[2,768,768]{2,1,0:T(8,128)} %get-tuple-element.397, f32[2,256,256]{2,1,0:T(8,128)S(1)} %get-tuple-element.383, s32[]{:T(128)} %constant.116.clone.1..sunk, s32[]{:T(128)S(6)} %select_n.137, s32[]{:T(128)S(6)} %select_n.138) | dynamic-update-slice | bytes 1048580 | tf_op jit(solution)/shard_map/while/body/eval_jaxpr/dynamic_update_slice | solution.py:69
  264.4 2.5 fusion.184
  277.3 2.7 add_bitcast_fusion.2
  281.5 6.9 %dynamic_update_slice.10 = f32[2,768,768]{2,1,0:T(8,128)} dynamic-update-slice(f32[2,768,768]{2,1,0:T(8,128)} %get-tuple-element.397, f32[2,256,256]{2,1,0:T(8,128)S(1)} %get-tuple-element.383, s32[]{:T(128)} %constant.116.clone.1..sunk, s32[]{:T(128)S(6)} %select_n.137, s32[]{:T(128)S(6)} %select_n.138) | dynamic-update-slice | bytes 1048580 | tf_op jit(solution)/shard_map/while/body/eval_jaxpr/dynamic_update_slice | solution.py:69
  304.3 2.5 fusion.184
  317.2 2.7 add_bitcast_fusion.2
  321.4 6.6 %dynamic_update_slice.10 = f32[2,768,768]{2,1,0:T(8,128)} dynamic-update-slice(f32[2,768,768]{2,1,0:T(8,128)} %get-tuple-element.397, f32[2,256,256]{2,1,0:T(8,128)S(1)} %get-tuple-element.383, s32[]{:T(128)} %constant.116.clone.1..sunk, s32[]{:T(128)S(6)} %select_n.137, s32[]{:T(128)S(6)} %select_n.138) | dynamic-update-slice | bytes 1048580 | tf_op jit(solution)/shard_map/while/body/eval_jaxpr/dynamic_update_slice | solution.py:69
  343.9 2.5 fusion.184
  356.8 2.7 add_bitcast_fusion.2
  361.0 6.9 %dynamic_update_slice.10 = f32[2,768,768]{2,1,0:T(8,128)} dynamic-update-slice(f32[2,768,768]{2,1,0:T(8,128)} %get-tuple-element.397, f32[2,256,256]{2,1,0:T(8,128)S(1)} %get-tuple-element.383, s32[]{:T(128)} %constant.116.clone.1..sunk, s32[]{:T(128)S(6)} %select_n.137, s32[]{:T(128)S(6)} %select_n.138) | dynamic-update-slice | bytes 1048580 | tf_op jit(solution)/shard_map/while/body/eval_jaxpr/dynamic_update_slice | solution.py:69
  369.6 7.0 %collective-permute-start.2 = (f32[2,768,256]{2,1,0:T(8,128)S(1)}, f32[2,768,256]{2,1,0:T(8,128)S(1)}, u32[]{:S(2)}, u32[]{:S(2)}) collective-permute-start(f32[2,768,256]{2,1,0:T(8,128)S(1)} %slice.116), channel_id=1, source_target_pairs={{0,1},{1,2},{2,3},{3,4},{4,5},{5,6},{6,7},{8,9},{9,10},{10,11},{11... | collective-permute-start | bytes 4718600 | tf_op jit(solution)/shard_map/ppermute | solution.py:12
  378.9 24.8 %collective-permute-done.2 = f32[2,768,256]{2,1,0:T(8,128)S(1)} collective-permute-done((f32[2,768,256]{2,1,0:T(8,128)S(1)}, f32[2,768,256]{2,1,0:T(8,128)S(1)}, u32[]{:S(2)}, u32[]{:S(2)}) %collective-permute-start.2) | collective-permute-done | bytes 1572896 | tf_op jit(solution)/shard_map/ppermute | solution.py:12
  407.1 9.8 %collective-permute-start.3 = (f32[2,256,512]{2,1,0:T(8,128)S(1)}, f32[2,256,512]{2,1,0:T(8,128)S(1)}, u32[]{:S(2)}, u32[]{:S(2)}) collective-permute-start(f32[2,256,512]{2,1,0:T(8,128)S(1)} %slice.135), channel_id=1, source_target_pairs={{0,8},{8,16},{16,24},{1,9},{9,17},{17,25},{2,10},{10,18},{18,26},{... | collective-permute-start | bytes 3145736 | tf_op jit(solution)/shard_map/ppermute | solution.py:12
  416.9 71.6 %all-reduce.3.cloned.1.call-done = f32[2,256,256]{2,1,0:T(8,128)} async-done(((f32[2,256,256]{2,1,0:T(8,128)}), f32[2,256,256]{2,1,0:T(8,128)}) %all-reduce.3.cloned.1.call-update) | async-done | bytes 524304 | tf_op jit(solution)/shard_map/psum | solution.py:78
  488.5 34.9 %all-reduce.5.cloned.1.call-done = f32[2,256,256]{2,1,0:T(8,128)} async-done(((f32[2,256,256]{2,1,0:T(8,128)}), f32[2,256,256]{2,1,0:T(8,128)}) %all-reduce.5.cloned.1.call-update) | async-done | bytes 524304 | tf_op jit(solution)/shard_map/psum | solution.py:79
  (179 shorter events, 217.7 us)
Async XLA Ops:
  7.2 2.8 copy-start.4
  7.2 481.3 %all-reduce.3.cloned.1.call-start = ((), (), s32[]{:S(2)}) async-start(), calls=%async_computation | async-start | bytes 1048576 | tf_op jit(solution)/shard_map/psum | solution.py:78
  8.7 4.6 collective-permute-start
  13.3 2.2 copy-start.3
  15.5 29.0 %collective-permute-start.1 = (f32[2,768,256]{2,1,0:T(8,128)}, f32[2,768,256]{2,1,0:T(8,128)S(1)}, u32[]{:S(2)}, u32[]{:S(2)}) collective-permute-start(f32[2,768,256]{2,1,0:T(8,128)} %slice.132), channel_id=1, source_target_pairs={{1,0},{2,1},{3,2},{4,3},{5,4},{6,5},{7,6},{9,8},{10,9},{11,10},{12... | collective-permute-start | bytes 4718600 | tf_op jit(solution)/shard_map/ppermute | solution.py:12
  48.9 2.5 copy-start
  48.9 2.5 copy-start.6
  367.9 11.0 %copy-start.1 = (f32[2,256,256]{2,1,0:T(8,128)}, f32[2,256,256]{2,1,0:T(8,128)S(1)}, u32[]{:S(2)}) copy-start(f32[2,256,256]{2,1,0:T(8,128)S(1)} %get-tuple-element.224) | copy-start | bytes 1572868
  369.6 34.0 %collective-permute-start.2 = (f32[2,768,256]{2,1,0:T(8,128)S(1)}, f32[2,768,256]{2,1,0:T(8,128)S(1)}, u32[]{:S(2)}, u32[]{:S(2)}) collective-permute-start(f32[2,768,256]{2,1,0:T(8,128)S(1)} %slice.116), channel_id=1, source_target_pairs={{0,1},{1,2},{2,3},{3,4},{4,5},{5,6},{6,7},{8,9},{9,10},{10,11},{11... | collective-permute-start | bytes 4718600 | tf_op jit(solution)/shard_map/ppermute | solution.py:12
  405.3 1.7 copy-start.2
  407.1 120.0 %collective-permute-start.3 = (f32[2,256,512]{2,1,0:T(8,128)S(1)}, f32[2,256,512]{2,1,0:T(8,128)S(1)}, u32[]{:S(2)}, u32[]{:S(2)}) collective-permute-start(f32[2,256,512]{2,1,0:T(8,128)S(1)} %slice.135), channel_id=1, source_target_pairs={{0,8},{8,16},{16,24},{1,9},{9,17},{17,25},{2,10},{10,18},{18,26},{... | collective-permute-start | bytes 3145736 | tf_op jit(solution)/shard_map/ppermute | solution.py:12
  416.8 106.6 %all-reduce.5.cloned.1.call-start = ((), (), s32[]{:S(2)}) async-start(), calls=%async_computation.1 | async-start | bytes 1048576 | tf_op jit(solution)/shard_map/psum | solution.py:79
  528.5 1.3 copy-start.5
Sparse Core Ops, SparseCore 0:
  417.0 71.4 all-reduce.2
  490.9 32.4 all-reduce.4
where the time goes:
time: 540 us; the launch traced here: 537 us
  matrix products  207 us (38%)
  waiting for transfers between devices  162 us (30%)
  local copies, waits for them, and re-layouts  72.3 us (13%)
  other arithmetic  32.1 us (6%)
  loops' own time  29.7 us (6%)
  starting transfers between devices  19.4 us (4%)
  between operations  14.2 us (3%)
    dot_general x128, matrix products, matmul(): jnp.dot(left, right, precision=lax.Precision.HIGHEST, preferred_element_t...  207 us
    psum x1, waiting for transfers between devices, shards(): partial_total = lax.psum(probe_acc, 'col')  71.6 us
    ppermute x4, waiting for transfers between devices, passed_along(): lax.ppermute(value, axis, [(source, source + steps) for source in range(f...  55.5 us
    dynamic_update_slice x8, local copies, waits for them, and re-layouts, step(): grad = lax.dynamic_update_slice(grad, old + obj_term, (zero, top, left))  52.5 us
    psum x1, waiting for transfers between devices, shards(): probe_total = lax.psum(partial_total, 'row')  34.9 us
    another operation x1, loops' own time, shards(): grad, probe_acc = lax.fori_loop(0, positions, step, start)  29.7 us
    ppermute x4, starting transfers between devices, passed_along(): lax.ppermute(value, axis, [(source, source + steps) for source in range(f...  19.4 us
    add x8, other arithmetic, step(): grad = lax.dynamic_update_slice(grad, old + obj_term, (zero, top, left))  11.9 us
  transfers between devices with their start and end apart: 6, of which 5 were waited for; matrix products, arithmetic and copies ran while one was open for 1% of the time, Pallas kernels for 0%

commit v1 on v0

v1 whole, which is shorter than its diff:
```python
import functools
import math

import jax
import jax.numpy as jnp
import ml_dtypes
import numpy as np
from jax import lax
from jax.experimental import pallas as pl
from jax.experimental.pallas import tpu as pltpu
from jax.sharding import PartitionSpec as P

LANES = 128
SUBLANES = 8
GROUP = 2


def passed_along(value, axis, steps):
    count = lax.axis_size(axis)
    first, last = (max(0, -steps), min(count, count - steps))
    return lax.ppermute(value, axis, [(source, source + steps) for source in range(first, last)])


def halves_np(table):
    high = table.astype(ml_dtypes.bfloat16)
    low = (table - high.astype(np.float64)).astype(ml_dtypes.bfloat16)
    return high, low


def tables(size):
    index = np.arange(size)
    angle = (index[:, None] * index[None, :] % size) * (2.0 * math.pi / size)
    cosine, sine = np.cos(angle) / math.sqrt(size), np.sin(angle) / math.sqrt(size)
    left, right = [], []
    for table in (cosine, sine - cosine, cosine + sine):
        high, low = halves_np(table)
        left.append(np.concatenate([high, high, low], axis=1))
        right.append(np.concatenate([high, low, high], axis=0))
    return np.stack(left), np.stack(right)


def halves(value):
    high = value.astype(jnp.bfloat16)
    return high, (value - high.astype(jnp.float32)).astype(jnp.bfloat16)


def from_left(table, value):
    high, low = halves(value)
    return jnp.dot(table, jnp.concatenate([high, low, high], axis=0), preferred_element_type=jnp.float32)


def from_right(table, value):
    high, low = halves(value)
    return jnp.dot(jnp.concatenate([high, high, low], axis=1), table, preferred_element_type=jnp.float32)


def transform(real, imag, left, right, forward):
    for product, table in ((from_left, left), (from_right, right)):
        shared = product(table[0], real + imag)
        if forward:
            real, imag = shared + product(table[1], imag), shared - product(table[2], real)
        else:
            real, imag = shared - product(table[2], imag), shared + product(table[1], real)
    return real, imag


def kernel(dims, off, obj, below, right_top, right_low, corner, probe, amp, left_t, right_t,
           g_main, g_below, g_right_top, g_right_low, g_corner, probe_acc, ext, grad, sems):
    side, rows, cols = dims
    step = pl.program_id(0)

    def pieces(buf):
        return (
            buf.at[:, pl.ds(0, rows), pl.ds(0, cols)],
            buf.at[:, pl.ds(rows, side), pl.ds(0, cols)],
            buf.at[:, pl.ds(0, side), pl.ds(cols, side)],
            buf.at[:, pl.ds(side, rows - side), pl.ds(cols, side)],
            buf.at[:, pl.ds(rows, side), pl.ds(cols, side)],
        )

    @pl.when(step == 0)
    def _():
        copies = [
            pltpu.make_async_copy(source, place, sems.at[number])
            for number, (source, place) in enumerate(
                zip((obj, below, right_top, right_low, corner), pieces(ext))
            )
        ]
        for copy in copies:
            copy.start()
        grad[...] = jnp.zeros_like(grad)
        probe_acc[...] = jnp.zeros_like(probe_acc)
        for copy in copies:
            copy.wait()

    wide, tall = side + LANES, side + SUBLANES
    probe_r, probe_i = probe[0], probe[1]
    found = []
    for item in range(GROUP):
        top = off[0, 0, step * GROUP + item, 0]
        at = off[0, 0, step * GROUP + item, 1]
        base = pl.multiple_of(at // LANES * LANES, LANES)
        shift = at - base
        start = pl.multiple_of(top // SUBLANES * SUBLANES, SUBLANES)
        drop = top - start

        def view_of(part):
            window = ext[part, pl.ds(start, tall), pl.ds(base, wide)]
            window = pltpu.roll(window, lax.rem(wide - shift, wide), 1)[:, :side]
            return pltpu.roll(window, lax.rem(tall - drop, tall), 0)[:side]

        view_r, view_i = view_of(0), view_of(1)
        wave_r = probe_r * view_r - probe_i * view_i
        wave_i = probe_r * view_i + probe_i * view_r
        far_r, far_i = transform(wave_r, wave_i, left_t, right_t, True)
        keep = 1.0 - amp[item] * lax.rsqrt(jnp.maximum(far_r * far_r + far_i * far_i, 0.25))
        chi_r, chi_i = transform(far_r * keep, far_i * keep, left_t, right_t, False)
        found.append((start, drop, base, shift, view_r, view_i, chi_r, chi_i))
    for start, drop, base, shift, view_r, view_i, chi_r, chi_i in found:
        terms = (probe_r * chi_r + probe_i * chi_i, probe_r * chi_i - probe_i * chi_r)
        for part in range(2):
            term = jnp.concatenate([terms[part], jnp.zeros((SUBLANES, side), jnp.float32)], axis=0)
            term = pltpu.roll(term, drop, 0)
            term = jnp.concatenate([term, jnp.zeros((tall, LANES), jnp.float32)], axis=1)
            grad[part, pl.ds(start, tall), pl.ds(base, wide)] += pltpu.roll(term, shift, 1)
        probe_acc[0] += view_r * chi_r + view_i * chi_i
        probe_acc[1] += view_r * chi_i - view_i * chi_r

    @pl.when(step == pl.num_programs(0) - 1)
    def _():
        copies = [
            pltpu.make_async_copy(place, target, sems.at[number])
            for number, (place, target) in enumerate(
                zip(pieces(grad), (g_main, g_below, g_right_top, g_right_low, g_corner))
            )
        ]
        for copy in copies:
            copy.start()
        for copy in copies:
            copy.wait()


def all_positions(offsets, obj, below, right_top, right_low, corner, probe, amp):
    side, rows, cols = probe.shape[1], obj.shape[1], obj.shape[2]
    count = offsets.shape[2]
    left_t, right_t = tables(side)
    anywhere = pl.BlockSpec(memory_space=pl.ANY)
    whole = lambda *shape: pl.BlockSpec(shape, lambda step: (0,) * len(shape))
    f32 = jnp.float32
    shape = lambda *dims: jax.ShapeDtypeStruct(dims, f32)
    return pl.pallas_call(
        functools.partial(kernel, (side, rows, cols)),
        grid=(count // GROUP,),
        in_specs=[pl.BlockSpec(memory_space=pltpu.SMEM)] + [anywhere] * 5 + [
            whole(2, side, side),
            pl.BlockSpec((GROUP, side, side), lambda step: (step, 0, 0)),
            whole(*left_t.shape),
            whole(*right_t.shape),
        ],
        out_specs=[anywhere] * 5 + [whole(2, side, side)],
        out_shape=[
            shape(2, rows, cols),
            shape(2, side, cols),
            shape(2, side, side),
            shape(2, rows - side, side),
            shape(2, side, side),
            shape(2, side, side),
        ],
        scratch_shapes=[
            pltpu.VMEM((2, rows + side, cols + side), f32),
            pltpu.VMEM((2, rows + side, cols + side), f32),
            pltpu.SemaphoreType.DMA((5,)),
        ],
        compiler_params=pltpu.CompilerParams(vmem_limit_bytes=44 * 2**20),
        cost_estimate=pl.CostEstimate(
            flops=count * 36 * 2 * side**3, bytes_accessed=12 * 2**20, transcendentals=0
        ),
    )(offsets, obj, below, right_top, right_low, corner, probe, amp,
      jnp.asarray(left_t), jnp.asarray(right_t))


def shards(object_field, probe, amplitude, offsets):
    rows, cols = object_field.shape[1:]
    side = probe.shape[1]
    positions = offsets.shape[2]
    right_top = passed_along(object_field[:, :side, :side], "col", -1)
    right_low = passed_along(object_field[:, side:, :side], "col", -1)
    below = passed_along(object_field[:, :side, :], "row", -1)
    corner = passed_along(right_top, "row", -1)
    g_main, g_below, g_top, g_low, g_corner, probe_acc = all_positions(
        offsets, object_field, below, right_top, right_low, corner, probe,
        amplitude.reshape(amplitude.shape[2:]),
    )
    got_corner = passed_along(g_corner, "row", 1)
    got_low = passed_along(g_low, "col", 1)
    got_rows = passed_along(g_below, "row", 1)
    got_top = passed_along(g_top + got_corner, "col", 1)
    pad = lambda value, top: jnp.pad(
        value, ((0, 0), (top, rows - top - value.shape[1]), (0, cols - value.shape[2]))
    )
    object_grad = g_main + pad(got_rows, 0) + pad(got_top, 0) + pad(got_low, side)
    count = positions * lax.axis_size("row") * lax.axis_size("col")
    probe_total = lax.psum(probe_acc, ("row", "col"))
    return (object_grad, probe_total / count)


def solution(mesh):
    placed = (
        P(None, "row", "col"),
        P(),
        P("row", "col", None, None, None),
        P("row", "col", None, None),
    )
    return jax.shard_map(
        shards, mesh=mesh, in_specs=placed, out_specs=(P(None, "row", "col"), P()), check_vma=False
    )
```

time: 540 us -> 227 us (0.42)
  matrix products: 207 us -> 0 us
  local copies, waits for them, and re-layouts: 72.3 us -> 12.5 us
  loops' own time: 29.7 us -> 0 us
  other arithmetic: 32.1 us -> 6.26 us
  Pallas kernels: 0 us -> 25.8 us
  waiting for transfers between devices: 162 us -> 149 us
    dot_general x128 -> x0, matrix products: 207 us -> none  [matmul(): jnp.dot(left, right, precision=lax.Precision.HIGHEST, preferred_element_t...]
    dynamic_update_slice x8 -> x0, local copies, waits for them, and re-layouts: 52.5 us -> none  [step(): grad = lax.dynamic_update_slice(grad, old + obj_term, (zero, top, left))]
    ppermute x4 -> x8, waiting for transfers between devices: 55.5 us -> 19.7 us  [passed_along(): lax.ppermute(value, axis, [(source, source + steps) for source in range(f...]
    another operation x1 -> x0, loops' own time: 29.7 us -> none  [shards(): grad, probe_acc = lax.fori_loop(0, positions, step, start)]
    pallas_call x0 -> x1, Pallas kernels: none -> 25.8 us  [all_positions(): pl.pallas_call(functools.partial(kernel, (side, rows, cols)), grid=(count...]
    psum x2 -> x1, waiting for transfers between devices: 106 us -> 129 us  [shards(): probe_total = lax.psum(probe_acc, ('row', 'col'))]
    add x16 -> x2, other arithmetic: 22.7 us -> 4.39 us  [the longest x1 3.53 us: shards(): g_main + pad(got_rows, 0) + pad(got_top, 0) + pad(got_low, side)]
    slice x13 -> x1, local copies, waits for them, and re-layouts: 11.4 us -> 2.15 us  [shards(): right_low = passed_along(object_field[:, side:, :side], 'col', -1)]
  transfers between devices with their start and end apart: 6 -> 9, of which waited for: 5 -> 3; matrix products, arithmetic and copies ran while one was open for 1% -> 2% of each run, Pallas kernels for 0% -> 0%
where the time goes in v1:
time: 227 us; the launch traced here: 226 us
  waiting for transfers between devices  149 us (66%)
  Pallas kernels  25.8 us (11%)
  starting transfers between devices  18.4 us (8%)
  between operations  14.1 us (6%)
  local copies, waits for them, and re-layouts  12.5 us (6%)
  other arithmetic  6.26 us (3%)
    psum x1, waiting for transfers between devices, shards(): probe_total = lax.psum(probe_acc, ('row', 'col'))  129 us
    pallas_call x1, Pallas kernels, all_positions(): pl.pallas_call(functools.partial(kernel, (side, rows, cols)), grid=(count...  25.8 us
    ppermute x8, waiting for transfers between devices, passed_along(): lax.ppermute(value, axis, [(source, source + steps) for source in range(f...  19.7 us
    ppermute x8, starting transfers between devices, passed_along(): lax.ppermute(value, axis, [(source, source + steps) for source in range(f...  18.4 us
    unnamed x21, local copies, waits for them, and re-layouts  8.13 us
  transfers between devices with their start and end apart: 9, of which 3 were waited for; matrix products, arithmetic and copies ran while one was open for 2% of the time, Pallas kernels for 0%

profile of v1, /device:TPU:0, one launch (start us, length us, event | category | flops | bytes accessed | tf_op | source)
XLA Modules:
  0.0 226.2 jit_solution(5250097891544555270)
XLA Ops:
  7.2 0.0 all-reduce.5.cloned.1.call-start
  7.2 2.2 fusion
  9.4 1.3 collective-permute-start.1
  10.7 2.3 %slice.9 = f32[2,256,512]{2,1,0:T(8,128)} slice(f32[2,512,512]{2,1,0:T(8,128)} %obj.1), slice={[0:2], [0:256], [0:512]} | slice | bytes 2097152 | tf_op jit(solution)/shard_map/slice | solution.py:188
  12.9 1.3 collective-permute-start
  14.2 1.3 collective-permute-start.2
  15.5 11.5 %collective-permute-done.1.right_top = f32[2,256,256]{2,1,0:T(8,128)S(1)} collective-permute-done((f32[2,256,256]{2,1,0:T(8,128)S(1)}, f32[2,256,256]{2,1,0:T(8,128)S(1)}, u32[]{:S(2)}, u32[]{:S(2)}) %collective-permute-start.1) | collective-permute-done | bytes 524320 | tf_op jit(solution)/shard_map/ppermute | solution.py:21
  27.0 1.3 collective-permute-start.3
  28.3 0.8 copy-done.1
  29.1 0.1 copy.8.off
  29.2 8.2 %collective-permute-done.2.right_low = f32[2,256,256]{2,1,0:T(8,128)S(1)} collective-permute-done((f32[2,256,256]{2,1,0:T(8,128)}, f32[2,256,256]{2,1,0:T(8,128)S(1)}, u32[]{:S(2)}, u32[]{:S(2)}) %collective-permute-start.2) | collective-permute-done | bytes 524320 | tf_op jit(solution)/shard_map/ppermute | solution.py:21
  37.4 0.8 copy-done.3
  38.2 0.8 copy-done.5
  39.0 0.0 collective-permute-done.below
  39.0 1.0 copy-done.2
  40.0 1.0 copy-done.4
  41.1 1.0 copy-done.6
  42.1 1.3 copy-done.7
  43.4 1.3 copy-done.8
  44.7 25.8 %shard_map.77 = (f32[2,512,512]{2,1,0:T(8,128)}, f32[2,256,512]{2,1,0:T(8,128)S(1)}, f32[2,256,256]{2,1,0:T(8,128)S(1)}, f32[2,256,256]{2,1,0:T(8,128)S(1)}, f32...) custom-call(s32[1,1,8,2]{3,2,1,0:T(8,128)S(1)} %copy.8.off, f32[2,512,512]{2,1,0:T(8,128)} %obj.1, ...), custom_call_target="tpu_custom_call" | custom-call | flops 9663676416 | bytes 12582912 | tf_op jit(solution)/shard_map/pallas_call | solution.py:151
  70.4 1.6 collective-permute-start.5
  72.1 4.1 %collective-permute-start.4 = (f32[2,256,512]{2,1,0:T(8,128)S(1)}, f32[2,256,512]{2,1,0:T(8,128)S(1)}, u32[]{:S(2)}, u32[]{:S(2)}) collective-permute-start(f32[2,256,512]{2,1,0:T(8,128)S(1)} %get-tuple-element.9), channel_id=1, source_target_pairs={{0,8},{8,16},{16,24},{1,9},{9,17},{17,25},{2,10},{10,18},{18,26},{... | collective-permute-start | bytes 3145736 | tf_op jit(solution)/shard_map/ppermute | solution.py:21
  76.1 4.3 %collective-permute-start.7 = (f32[2,256,256]{2,1,0:T(8,128)S(1)}, f32[2,256,256]{2,1,0:T(8,128)S(1)}, u32[]{:S(2)}, u32[]{:S(2)}) collective-permute-start(f32[2,256,256]{2,1,0:T(8,128)S(1)} %get-tuple-element.12), channel_id=1, source_target_pairs={{0,1},{1,2},{2,3},{3,4},{4,5},{5,6},{6,7},{8,9},{9,10},{10,11},{11... | collective-permute-start | bytes 1572872 | tf_op jit(solution)/shard_map/ppermute | solution.py:21
  80.4 0.0 collective-permute-done.5
  80.4 0.9 add.21
  81.3 3.3 %collective-permute-start.6 = (f32[2,256,256]{2,1,0:T(8,128)}, f32[2,256,256]{2,1,0:T(8,128)}, u32[]{:S(2)}, u32[]{:S(2)}) collective-permute-start(f32[2,256,256]{2,1,0:T(8,128)} %add.21), channel_id=1, source_target_pairs={{0,1},{1,2},{2,3},{3,4},{4,5},{5,6},{6,7},{8,9},{9,10},{10,11},{11... | collective-permute-start | bytes 1572872 | tf_op jit(solution)/shard_map/ppermute | solution.py:21
  84.6 0.0 all-reduce.5.cloned.1.call-update
  84.6 129.4 %all-reduce.5.cloned.1.call-done = f32[2,256,256]{2,1,0:T(8,128)} async-done(((f32[2,256,256]{2,1,0:T(8,128)}), f32[2,256,256]{2,1,0:T(8,128)}) %all-reduce.5.cloned.1.call-update) | async-done | bytes 524304 | tf_op jit(solution)/shard_map/psum | solution.py:203
  214.0 1.9 broadcast_multiply_fusion
  215.8 0.0 collective-permute-done.7
  215.8 0.0 collective-permute-done.6
  215.9 3.5 %pad_add_fusion = f32[2,512,512]{2,1,0:T(8,128)} fusion(f32[2,256,256]{2,1,0:T(8,128)S(1)} %collective-permute-done.7, f32[2,256,256]{2,1,0:T(8,128)} %collective-permute-done.6, f32[2,512,512]{2,1,0:T(8,128)} %get-tuple-element.8, f32[2,256,512]{2,1,0:T(8,128)S(1)} %collective-permute-done.4), kind=kLoop, calls=%fused_computation | loop fusion | flops 1572864 | bytes 6291456 | tf_op jit(solution)/shard_map/add | solution.py:201
  (14 shorter events, 0.0 us)
Async XLA Ops:
  7.2 21.9 %copy-start.9 = (s32[1,1,8,2]{2,3,1,0:T(2,128)S(1)}, s32[1,1,8,2]{2,3,1,0:T(2,128)}, u32[]{:S(2)}) copy-start(s32[1,1,8,2]{2,3,1,0:T(2,128)} %param.9) | copy-start | bytes 196
  7.2 31.8 %copy-start = (f32[2,256,256]{2,1,0:T(8,128)S(1)}, f32[2,256,256]{2,1,0:T(8,128)}, u32[]{:S(2)}) copy-start(f32[2,256,256]{2,1,0:T(8,128)} %probe.1) | copy-start | bytes 1572868
  7.2 206.8 %all-reduce.5.cloned.1.call-start = ((), (), s32[]{:S(2)}) async-start(), calls=%async_computation | async-start | bytes 1048576 | tf_op jit(solution)/shard_map/psum | solution.py:203
  9.4 17.6 %collective-permute-start.1 = (f32[2,256,256]{2,1,0:T(8,128)S(1)}, f32[2,256,256]{2,1,0:T(8,128)S(1)}, u32[]{:S(2)}, u32[]{:S(2)}) collective-permute-start(f32[2,256,256]{2,1,0:T(8,128)S(1)} %get-tuple-element.15), channel_id=1, source_target_pairs={{1,0},{2,1},{3,2},{4,3},{5,4},{6,5},{7,6},{9,8},{10,9},{11,10},{12... | collective-permute-start | bytes 1572872 | tf_op jit(solution)/shard_map/ppermute | solution.py:21
  12.9 26.1 %collective-permute-start = (f32[2,256,512]{2,1,0:T(8,128)}, f32[2,256,512]{2,1,0:T(8,128)S(1)}, u32[]{:S(2)}, u32[]{:S(2)}) collective-permute-start(f32[2,256,512]{2,1,0:T(8,128)} %slice.9), channel_id=1, source_target_pairs={{8,0},{16,8},{24,16},{9,1},{17,9},{25,17},{10,2},{18,10},{26,18},{... | collective-permute-start | bytes 3145736 | tf_op jit(solution)/shard_map/ppermute | solution.py:21
  14.2 23.2 %collective-permute-start.2 = (f32[2,256,256]{2,1,0:T(8,128)}, f32[2,256,256]{2,1,0:T(8,128)S(1)}, u32[]{:S(2)}, u32[]{:S(2)}) collective-permute-start(f32[2,256,256]{2,1,0:T(8,128)} %get-tuple-element.14), channel_id=1, source_target_pairs={{1,0},{2,1},{3,2},{4,3},{5,4},{6,5},{7,6},{9,8},{10,9},{11,10},{12... | collective-permute-start | bytes 1572872 | tf_op jit(solution)/shard_map/ppermute | solution.py:21
  27.0 11.2 %collective-permute-start.3 = (f32[2,256,256]{2,1,0:T(8,128)S(1)}, f32[2,256,256]{2,1,0:T(8,128)S(1)}, u32[]{:S(2)}, u32[]{:S(2)}) collective-permute-start(f32[2,256,256]{2,1,0:T(8,128)S(1)} %collective-permute-done.1.right_top), channel_id=1, source_target_pairs={{8,0},{16,8},{24,16},{9,1},{17,9},{25,17},{10,2},{18,10},{26,18},{... | collective-permute-start | bytes 1572872 | tf_op jit(solution)/shard_map/ppermute | solution.py:21
  28.3 0.8 copy-start.1
  37.4 0.8 copy-start.3
  38.2 0.8 copy-start.5
  39.0 1.0 copy-start.2
  40.0 1.0 copy-start.4
  41.1 1.0 copy-start.6
  42.1 1.3 copy-start.7
  43.4 1.3 copy-start.8
  70.4 10.0 %collective-permute-start.5 = (f32[2,256,256]{2,1,0:T(8,128)S(1)}, f32[2,256,256]{2,1,0:T(8,128)S(1)}, u32[]{:S(2)}, u32[]{:S(2)}) collective-permute-start(f32[2,256,256]{2,1,0:T(8,128)S(1)} %get-tuple-element.11), channel_id=1, source_target_pairs={{0,8},{8,16},{16,24},{1,9},{9,17},{17,25},{2,10},{10,18},{18,26},{... | collective-permute-start | bytes 1572872 | tf_op jit(solution)/shard_map/ppermute | solution.py:21
  72.1 143.8 %collective-permute-start.4 = (f32[2,256,512]{2,1,0:T(8,128)S(1)}, f32[2,256,512]{2,1,0:T(8,128)S(1)}, u32[]{:S(2)}, u32[]{:S(2)}) collective-permute-start(f32[2,256,512]{2,1,0:T(8,128)S(1)} %get-tuple-element.9), channel_id=1, source_target_pairs={{0,8},{8,16},{16,24},{1,9},{9,17},{17,25},{2,10},{10,18},{18,26},{... | collective-permute-start | bytes 3145736 | tf_op jit(solution)/shard_map/ppermute | solution.py:21
  76.1 139.7 %collective-permute-start.7 = (f32[2,256,256]{2,1,0:T(8,128)S(1)}, f32[2,256,256]{2,1,0:T(8,128)S(1)}, u32[]{:S(2)}, u32[]{:S(2)}) collective-permute-start(f32[2,256,256]{2,1,0:T(8,128)S(1)} %get-tuple-element.12), channel_id=1, source_target_pairs={{0,1},{1,2},{2,3},{3,4},{4,5},{5,6},{6,7},{8,9},{9,10},{10,11},{11... | collective-permute-start | bytes 1572872 | tf_op jit(solution)/shard_map/ppermute | solution.py:21
  81.3 134.5 %collective-permute-start.6 = (f32[2,256,256]{2,1,0:T(8,128)}, f32[2,256,256]{2,1,0:T(8,128)}, u32[]{:S(2)}, u32[]{:S(2)}) collective-permute-start(f32[2,256,256]{2,1,0:T(8,128)} %add.21), channel_id=1, source_target_pairs={{0,1},{1,2},{2,3},{3,4},{4,5},{5,6},{6,7},{8,9},{9,10},{10,11},{11... | collective-permute-start | bytes 1572872 | tf_op jit(solution)/shard_map/ppermute | solution.py:21
Sparse Core Ops, SparseCore 0:
  84.7 129.1 all-reduce.4

commit v2 on v1

--- a/solution.py
+++ b/solution.py
@@ -19,6 +19,40 @@
     count = lax.axis_size(axis)
     first, last = (max(0, -steps), min(count, count - steps))
     return lax.ppermute(value, axis, [(source, source + steps) for source in range(first, last)])
+
+
+def bit_partners(axis):
+    count = lax.axis_size(axis)
+    return [(axis, 1 << power) for power in range(count.bit_length() - 1)]
+
+
+def swapped(value, axis, bit):
+    return lax.ppermute(value, axis, [(at, at ^ bit) for at in range(lax.axis_size(axis))])
+
+
+def summed_over(value, axes):
+    if any(lax.axis_size(axis) & (lax.axis_size(axis) - 1) for axis in axes):
+        return lax.psum(value, axes)
+    rounds = [pair for axis in axes for pair in bit_partners(axis)]
+    shape = value.shape
+    value = value.reshape(-1, shape[-1])
+    split = []
+    for axis, bit in rounds:
+        half = value.shape[0] // 2
+        if len(split) < 3 and half % SUBLANES == 0:
+            upper = (lax.axis_index(axis) & bit) // bit
+            kept = lax.dynamic_slice_in_dim(value, upper * half, half, 0)
+            sent = lax.dynamic_slice_in_dim(value, (1 - upper) * half, half, 0)
+            value = kept + swapped(sent, axis, bit)
+            split.append((axis, bit, upper))
+        else:
+            value = value + swapped(value, axis, bit)
+    for axis, bit, upper in reversed(split):
+        other = swapped(value, axis, bit)
+        first = jnp.where(upper == 0, value, other)
+        second = jnp.where(upper == 0, other, value)
+        value = jnp.concatenate([first, second], axis=0)
+    return value.reshape(shape)
 
 
 def halves_np(table):
@@ -171,7 +205,7 @@
             pltpu.VMEM((2, rows + side, cols + side), f32),
             pltpu.SemaphoreType.DMA((5,)),
         ],
-        compiler_params=pltpu.CompilerParams(vmem_limit_bytes=44 * 2**20),
+        compiler_params=pltpu.CompilerParams(vmem_limit_bytes=56 * 2**20),
         cost_estimate=pl.CostEstimate(
             flops=count * 36 * 2 * side**3, bytes_accessed=12 * 2**20, transcendentals=0
         ),
@@ -200,7 +234,7 @@
     )
     object_grad = g_main + pad(got_rows, 0) + pad(got_top, 0) + pad(got_low, side)
     count = positions * lax.axis_size("row") * lax.axis_size("col")
-    probe_total = lax.psum(probe_acc, ("row", "col"))
+    probe_total = summed_over(probe_acc, ("row", "col"))
     return (object_grad, probe_total / count)
 
 

time: 227 us -> 128 us (0.56)
  waiting for transfers between devices: 149 us -> 54.6 us
  between operations: 14.1 us -> 0.83 us
  starting transfers between devices: 18.4 us -> 30.9 us
  local copies, waits for them, and re-layouts: 12.5 us -> 4.2 us
  other arithmetic: 6.26 us -> 8.59 us
  Pallas kernels: 25.8 us -> 28.1 us
    psum x1 -> x0, waiting for transfers between devices: 129 us -> none  [shards(): probe_total = lax.psum(probe_acc, ('row', 'col'))]
    ppermute x8, waiting for transfers between devices: 19.7 us -> 39.9 us  [passed_along(): lax.ppermute(value, axis, [(source, source + steps) for source in range(f...]
    ppermute x0 -> x8, waiting for transfers between devices: none -> 14.8 us  [swapped(): lax.ppermute(value, axis, [(at, at ^ bit) for at in range(lax.axis_size(a...]
    ppermute x0 -> x8, starting transfers between devices: none -> 13.9 us  [swapped(): lax.ppermute(value, axis, [(at, at ^ bit) for at in range(lax.axis_size(a...]
    unnamed x21 -> x11, local copies, waits for them, and re-layouts: 8.13 us -> 1.64 us
    pallas_call x1, Pallas kernels: 25.8 us -> 28.1 us  [all_positions(): pl.pallas_call(functools.partial(kernel, (side, rows, cols)), grid=(count...]
  transfers between devices with their start and end apart: 9 -> 16, of which waited for: 3 -> 10; matrix products, arithmetic and copies ran while one was open for 2% -> 4% of each run, Pallas kernels for 0% -> 0%
where the time goes in v2:
time: 128 us; the launch traced here: 127 us
  waiting for transfers between devices  54.6 us (43%)
  starting transfers between devices  30.9 us (24%)
  Pallas kernels  28.1 us (22%)
  other arithmetic  8.59 us (7%)
  local copies, waits for them, and re-layouts  4.2 us (3%)
    ppermute x8, waiting for transfers between devices, passed_along(): lax.ppermute(value, axis, [(source, source + steps) for source in range(f...  39.9 us
    pallas_call x1, Pallas kernels, all_positions(): pl.pallas_call(functools.partial(kernel, (side, rows, cols)), grid=(count...  28.1 us
    ppermute x8, starting transfers between devices, passed_along(): lax.ppermute(value, axis, [(source, source + steps) for source in range(f...  17 us
    ppermute x8, waiting for transfers between devices, swapped(): lax.ppermute(value, axis, [(at, at ^ bit) for at in range(lax.axis_size(a...  14.8 us
    ppermute x8, starting transfers between devices, swapped(): lax.ppermute(value, axis, [(at, at ^ bit) for at in range(lax.axis_size(a...  13.9 us
    add x1, other arithmetic, shards(): g_main + pad(got_rows, 0) + pad(got_top, 0) + pad(got_low, side)  2.93 us
  transfers between devices with their start and end apart: 16, of which 10 were waited for; matrix products, arithmetic and copies ran while one was open for 4% of the time, Pallas kernels for 0%

profile of v2, /device:TPU:0, one launch (start us, length us, event | category | flops | bytes accessed | tf_op | source)
XLA Modules:
  0.0 127.2 jit_solution(8031335701877926364)
XLA Ops:
  0.7 1.4 %slice.9 = f32[2,256,512]{2,1,0:T(8,128)S(1)} slice(f32[2,512,512]{2,1,0:T(8,128)} %obj.1), slice={[0:2], [0:256], [0:512]} | slice | bytes 2097152 | tf_op jit(solution)/shard_map/slice | solution.py:222
  2.1 1.3 %collective-permute-start = (f32[2,256,512]{2,1,0:T(8,128)S(1)}, f32[2,256,512]{2,1,0:T(8,128)S(1)}, u32[]{:S(2)}, u32[]{:S(2)}) collective-permute-start(f32[2,256,512]{2,1,0:T(8,128)S(1)} %slice.9), channel_id=1, source_target_pairs={{8,0},{16,8},{24,16},{9,1},{17,9},{25,17},{10,2},{18,10},{26,18},{... | collective-permute-start | bytes 3145736 | tf_op jit(solution)/shard_map/ppermute | solution.py:21
  3.5 1.3 %collective-permute-start.1 = (f32[2,256,256]{2,1,0:T(8,128)S(1)}, f32[2,256,256]{2,1,0:T(8,128)S(1)}, u32[]{:S(2)}, u32[]{:S(2)}) collective-permute-start(f32[2,256,256]{2,1,0:T(8,128)S(1)} %get-tuple-element.15), channel_id=1, source_target_pairs={{1,0},{2,1},{3,2},{4,3},{5,4},{6,5},{7,6},{9,8},{10,9},{11,10},{12... | collective-permute-start | bytes 1572872 | tf_op jit(solution)/shard_map/ppermute | solution.py:21
  4.8 1.3 %collective-permute-start.2 = (f32[2,256,256]{2,1,0:T(8,128)S(1)}, f32[2,256,256]{2,1,0:T(8,128)}, u32[]{:S(2)}, u32[]{:S(2)}) collective-permute-start(f32[2,256,256]{2,1,0:T(8,128)S(1)} %get-tuple-element.14), channel_id=1, source_target_pairs={{1,0},{2,1},{3,2},{4,3},{5,4},{6,5},{7,6},{9,8},{10,9},{11,10},{12... | collective-permute-start | bytes 1572872 | tf_op jit(solution)/shard_map/ppermute | solution.py:21
  6.1 14.7 %collective-permute-done.1.right_top = f32[2,256,256]{2,1,0:T(8,128)S(1)} collective-permute-done((f32[2,256,256]{2,1,0:T(8,128)S(1)}, f32[2,256,256]{2,1,0:T(8,128)S(1)}, u32[]{:S(2)}, u32[]{:S(2)}) %collective-permute-start.1) | collective-permute-done | bytes 524320 | tf_op jit(solution)/shard_map/ppermute | solution.py:21
  20.8 1.3 %collective-permute-start.3 = (f32[2,256,256]{2,1,0:T(8,128)S(1)}, f32[2,256,256]{2,1,0:T(8,128)}, u32[]{:S(2)}, u32[]{:S(2)}) collective-permute-start(f32[2,256,256]{2,1,0:T(8,128)S(1)} %collective-permute-done.1.right_top), channel_id=1, source_target_pairs={{8,0},{16,8},{24,16},{9,1},{17,9},{25,17},{10,2},{18,10},{26,18},{... | collective-permute-start | bytes 1572872 | tf_op jit(solution)/shard_map/ppermute | solution.py:21
  22.8 9.4 %collective-permute-done.2.right_low = f32[2,256,256]{2,1,0:T(8,128)} collective-permute-done((f32[2,256,256]{2,1,0:T(8,128)S(1)}, f32[2,256,256]{2,1,0:T(8,128)}, u32[]{:S(2)}, u32[]{:S(2)}) %collective-permute-start.2) | collective-permute-done | bytes 524320 | tf_op jit(solution)/shard_map/ppermute | solution.py:21
  32.2 0.9 copy-done.3
  33.1 28.1 %shard_map.77 = (f32[2,512,512]{2,1,0:T(8,128)}, f32[2,256,512]{2,1,0:T(8,128)}, f32[2,256,256]{2,1,0:T(8,128)}, f32[2,256,256]{2,1,0:T(8,128)}, f32[2,256,256]{2,1,0:T(8,128)}, /*index=5*/f32[2,256,256]{2,1,0:T(8,128)}) custom-call(s32[1,1,8,2]{3,2,1,0:T(8,128)} %copy.8.off, f32[2,512,512]{2,1,0:T(8,128)} %obj.1, f32[2,256,512]{2,1,0:T(8,128)} %copy-done.3, ...), custom_call_target="tpu_custom_call" | custom-call | flops 9663676416 | bytes 12582912 | tf_op jit(solution)/shard_map/pallas_call | solution.py:185
  61.2 1.0 constant_dynamic-slice_fusion.2
  62.5 1.2 collective-permute-done.8
  63.8 1.0 dynamic-slice_add_fusion
  64.8 2.7 %collective-permute-start.9 = (f32[128,256]{1,0:T(8,128)S(1)}, f32[128,256]{1,0:T(8,128)S(1)}, u32[]{:S(2)}, u32[]{:S(2)}) collective-permute-start(f32[128,256]{1,0:T(8,128)S(1)} %constant_dynamic-slice_fusion.1), channel_id=1, source_target_pairs={{0,16},{8,24},{16,0},{24,8},{1,17},{9,25},{17,1},{25,9},{2,18},{10... | collective-permute-start | bytes 393224 | tf_op jit(solution)/shard_map/ppermute | solution.py:30
  67.5 3.8 %collective-permute-done.9 = f32[128,256]{1,0:T(8,128)S(1)} collective-permute-done((f32[128,256]{1,0:T(8,128)S(1)}, f32[128,256]{1,0:T(8,128)S(1)}, u32[]{:S(2)}, u32[]{:S(2)}) %collective-permute-start.9) | collective-permute-done | bytes 131104 | tf_op jit(solution)/shard_map/ppermute | solution.py:30
  71.3 2.5 %collective-permute-start.10 = (f32[64,256]{1,0:T(8,128)S(1)}, f32[64,256]{1,0:T(8,128)S(1)}, u32[]{:S(2)}, u32[]{:S(2)}) collective-permute-start(f32[64,256]{1,0:T(8,128)S(1)} %constant_dynamic-slice_fusion), channel_id=1, source_target_pairs={{0,1},{1,0},{2,3},{3,2},{4,5},{5,4},{6,7},{7,6},{8,9},{9,8},{10,11... | collective-permute-start | bytes 196616 | tf_op jit(solution)/shard_map/ppermute | solution.py:30
  73.8 2.2 %collective-permute-done.10 = f32[64,256]{1,0:T(8,128)S(1)} collective-permute-done((f32[64,256]{1,0:T(8,128)S(1)}, f32[64,256]{1,0:T(8,128)S(1)}, u32[]{:S(2)}, u32[]{:S(2)}) %collective-permute-start.10) | collective-permute-done | bytes 65568 | tf_op jit(solution)/shard_map/ppermute | solution.py:30
  76.1 1.7 %collective-permute-start.11 = (f32[64,256]{1,0:T(8,128)S(1)}, f32[64,256]{1,0:T(8,128)S(1)}, u32[]{:S(2)}, u32[]{:S(2)}) collective-permute-start(f32[64,256]{1,0:T(8,128)S(1)} %dynamic-slice_add_fusion.2), channel_id=1, source_target_pairs={{0,2},{1,3},{2,0},{3,1},{4,6},{5,7},{6,4},{7,5},{8,10},{9,11},{10,... | collective-permute-start | bytes 196616 | tf_op jit(solution)/shard_map/ppermute | solution.py:30
  77.7 2.7 %collective-permute-done.11 = f32[64,256]{1,0:T(8,128)S(1)} collective-permute-done((f32[64,256]{1,0:T(8,128)S(1)}, f32[64,256]{1,0:T(8,128)S(1)}, u32[]{:S(2)}, u32[]{:S(2)}) %collective-permute-start.11) | collective-permute-done | bytes 65568 | tf_op jit(solution)/shard_map/ppermute | solution.py:30
  80.4 2.7 %collective-permute-start.12 = (f32[64,256]{1,0:T(8,128)S(1)}, f32[64,256]{1,0:T(8,128)S(1)}, u32[]{:S(2)}, u32[]{:S(2)}) collective-permute-start(f32[64,256]{1,0:T(8,128)S(1)} %add.67), channel_id=1, source_target_pairs={{0,4},{1,5},{2,6},{3,7},{4,0},{5,1},{6,2},{7,3},{8,12},{9,13},{10,... | collective-permute-start | bytes 196616 | tf_op jit(solution)/shard_map/ppermute | solution.py:30
  83.1 2.6 %collective-permute-done.12 = f32[64,256]{1,0:T(8,128)S(1)} collective-permute-done((f32[64,256]{1,0:T(8,128)S(1)}, f32[64,256]{1,0:T(8,128)S(1)}, u32[]{:S(2)}, u32[]{:S(2)}) %collective-permute-start.12) | collective-permute-done | bytes 65568 | tf_op jit(solution)/shard_map/ppermute | solution.py:30
  85.7 2.1 %collective-permute-start.13 = (f32[64,256]{1,0:T(8,128)S(1)}, f32[64,256]{1,0:T(8,128)S(1)}, u32[]{:S(2)}, u32[]{:S(2)}) collective-permute-start(f32[64,256]{1,0:T(8,128)S(1)} %add.68), channel_id=1, source_target_pairs={{0,1},{1,0},{2,3},{3,2},{4,5},{5,4},{6,7},{7,6},{8,9},{9,8},{10,11... | collective-permute-start | bytes 196616 | tf_op jit(solution)/shard_map/ppermute | solution.py:30
  87.8 2.2 %collective-permute-done.13 = f32[64,256]{1,0:T(8,128)S(1)} collective-permute-done((f32[64,256]{1,0:T(8,128)S(1)}, f32[64,256]{1,0:T(8,128)S(1)}, u32[]{:S(2)}, u32[]{:S(2)}) %collective-permute-start.13) | collective-permute-done | bytes 65568 | tf_op jit(solution)/shard_map/ppermute | solution.py:30
  90.1 1.9 %collective-permute-start.14 = (f32[128,256]{1,0:T(8,128)S(1)}, f32[128,256]{1,0:T(8,128)S(1)}, u32[]{:S(2)}, u32[]{:S(2)}) collective-permute-start(f32[128,256]{1,0:T(8,128)S(1)} %pad_maximum_fusion.1), channel_id=1, source_target_pairs={{0,16},{8,24},{16,0},{24,8},{1,17},{9,25},{17,1},{25,9},{2,18},{10... | collective-permute-start | bytes 393224 | tf_op jit(solution)/shard_map/ppermute | solution.py:30
  91.9 2.1 %collective-permute-start.5 = (f32[2,256,256]{2,1,0:T(8,128)}, f32[2,256,256]{2,1,0:T(8,128)}, u32[]{:S(2)}, u32[]{:S(2)}) collective-permute-start(f32[2,256,256]{2,1,0:T(8,128)} %get-tuple-element.11), channel_id=1, source_target_pairs={{0,8},{8,16},{16,24},{1,9},{9,17},{17,25},{2,10},{10,18},{18,26},{... | collective-permute-start | bytes 1572872 | tf_op jit(solution)/shard_map/ppermute | solution.py:21
  94.0 2.1 %collective-permute-start.4 = (f32[2,256,512]{2,1,0:T(8,128)}, f32[2,256,512]{2,1,0:T(8,128)S(1)}, u32[]{:S(2)}, u32[]{:S(2)}) collective-permute-start(f32[2,256,512]{2,1,0:T(8,128)} %get-tuple-element.9), channel_id=1, source_target_pairs={{0,8},{8,16},{16,24},{1,9},{9,17},{17,25},{2,10},{10,18},{18,26},{... | collective-permute-start | bytes 3145736 | tf_op jit(solution)/shard_map/ppermute | solution.py:21
  96.9 4.7 %collective-permute-start.7 = (f32[2,256,256]{2,1,0:T(8,128)}, f32[2,256,256]{2,1,0:T(8,128)}, u32[]{:S(2)}, u32[]{:S(2)}) collective-permute-start(f32[2,256,256]{2,1,0:T(8,128)} %get-tuple-element.12), channel_id=1, source_target_pairs={{0,1},{1,2},{2,3},{3,4},{4,5},{5,6},{6,7},{8,9},{9,10},{10,11},{11... | collective-permute-start | bytes 1572872 | tf_op jit(solution)/shard_map/ppermute | solution.py:21
  101.7 2.1 %add.55 = f32[2,256,256]{2,1,0:T(8,128)} add(f32[2,256,256]{2,1,0:T(8,128)} %get-tuple-element.10, f32[2,256,256]{2,1,0:T(8,128)} %collective-permute-done.5) | non-fusion elementwise | flops 131072 | bytes 1572864 | tf_op jit(solution)/shard_map/add | solution.py:231
  103.7 2.9 %collective-permute-start.6 = (f32[2,256,256]{2,1,0:T(8,128)}, f32[2,256,256]{2,1,0:T(8,128)}, u32[]{:S(2)}, u32[]{:S(2)}) collective-permute-start(f32[2,256,256]{2,1,0:T(8,128)} %add.55), channel_id=1, source_target_pairs={{0,1},{1,2},{2,3},{3,4},{4,5},{5,6},{6,7},{8,9},{9,10},{10,11},{11... | collective-permute-start | bytes 1572872 | tf_op jit(solution)/shard_map/ppermute | solution.py:21
  106.6 1.0 broadcast_select_fusion.1
  108.5 4.9 %collective-permute-done.7 = f32[2,256,256]{2,1,0:T(8,128)} collective-permute-done((f32[2,256,256]{2,1,0:T(8,128)}, f32[2,256,256]{2,1,0:T(8,128)}, u32[]{:S(2)}, u32[]{:S(2)}) %collective-permute-start.7) | collective-permute-done | bytes 524320 | tf_op jit(solution)/shard_map/ppermute | solution.py:21
  113.4 10.9 %collective-permute-done.6 = f32[2,256,256]{2,1,0:T(8,128)} collective-permute-done((f32[2,256,256]{2,1,0:T(8,128)}, f32[2,256,256]{2,1,0:T(8,128)}, u32[]{:S(2)}, u32[]{:S(2)}) %collective-permute-start.6) | collective-permute-done | bytes 524320 | tf_op jit(solution)/shard_map/ppermute | solution.py:21
  124.3 2.9 %pad_add_fusion = f32[2,512,512]{2,1,0:T(8,128)} fusion(f32[2,256,256]{2,1,0:T(8,128)} %collective-permute-done.7, f32[2,256,256]{2,1,0:T(8,128)} %collective-permute-done.6, f32[2,512,512]{2,1,0:T(8,128)S(1)} %copy-done, f32[2,256,512]{2,1,0:T(8,128)S(1)} %collective-permute-done.4), kind=kLoop, calls=%fused_computation | loop fusion | flops 1572864 | bytes 6291456 | tf_op jit(solution)/shard_map/add | solution.py:235
  (30 shorter events, 2.8 us)
Async XLA Ops:
  0.6 2.8 %copy-start.1 = (f32[2,512,512]{2,1,0:T(8,128)S(1)}, f32[2,512,512]{2,1,0:T(8,128)}, u32[]{:S(2)}) copy-start(f32[2,512,512]{2,1,0:T(8,128)} %obj.1) | copy-start | bytes 6291460
  0.6 21.5 %copy-start.2 = (s32[1,1,8,2]{2,3,1,0:T(2,128)S(1)}, s32[1,1,8,2]{2,3,1,0:T(2,128)}, u32[]{:S(2)}) copy-start(s32[1,1,8,2]{2,3,1,0:T(2,128)} %param.9) | copy-start | bytes 196
  2.1 30.1 %collective-permute-start = (f32[2,256,512]{2,1,0:T(8,128)S(1)}, f32[2,256,512]{2,1,0:T(8,128)S(1)}, u32[]{:S(2)}, u32[]{:S(2)}) collective-permute-start(f32[2,256,512]{2,1,0:T(8,128)S(1)} %slice.9), channel_id=1, source_target_pairs={{8,0},{16,8},{24,16},{9,1},{17,9},{25,17},{10,2},{18,10},{26,18},{... | collective-permute-start | bytes 3145736 | tf_op jit(solution)/shard_map/ppermute | solution.py:21
  3.5 17.3 %collective-permute-start.1 = (f32[2,256,256]{2,1,0:T(8,128)S(1)}, f32[2,256,256]{2,1,0:T(8,128)S(1)}, u32[]{:S(2)}, u32[]{:S(2)}) collective-permute-start(f32[2,256,256]{2,1,0:T(8,128)S(1)} %get-tuple-element.15), channel_id=1, source_target_pairs={{1,0},{2,1},{3,2},{4,3},{5,4},{6,5},{7,6},{9,8},{10,9},{11,10},{12... | collective-permute-start | bytes 1572872 | tf_op jit(solution)/shard_map/ppermute | solution.py:21
  4.8 27.3 %collective-permute-start.2 = (f32[2,256,256]{2,1,0:T(8,128)S(1)}, f32[2,256,256]{2,1,0:T(8,128)}, u32[]{:S(2)}, u32[]{:S(2)}) collective-permute-start(f32[2,256,256]{2,1,0:T(8,128)S(1)} %get-tuple-element.14), channel_id=1, source_target_pairs={{1,0},{2,1},{3,2},{4,3},{5,4},{6,5},{7,6},{9,8},{10,9},{11,10},{12... | collective-permute-start | bytes 1572872 | tf_op jit(solution)/shard_map/ppermute | solution.py:21
  20.8 11.4 %copy-start.4 = (f32[2,256,256]{2,1,0:T(8,128)}, f32[2,256,256]{2,1,0:T(8,128)S(1)}, u32[]{:S(2)}) copy-start(f32[2,256,256]{2,1,0:T(8,128)S(1)} %collective-permute-done.1.right_top) | copy-start | bytes 1572868
  20.8 11.3 %collective-permute-start.3 = (f32[2,256,256]{2,1,0:T(8,128)S(1)}, f32[2,256,256]{2,1,0:T(8,128)}, u32[]{:S(2)}, u32[]{:S(2)}) collective-permute-start(f32[2,256,256]{2,1,0:T(8,128)S(1)} %collective-permute-done.1.right_top), channel_id=1, source_target_pairs={{8,0},{16,8},{24,16},{9,1},{17,9},{25,17},{10,2},{18,10},{26,18},{... | collective-permute-start | bytes 1572872 | tf_op jit(solution)/shard_map/ppermute | solution.py:21
  32.2 1.0 copy-start.3
  62.2 1.6 %collective-permute-start.8 = (f32[256,256]{1,0:T(8,128)S(1)}, f32[256,256]{1,0:T(8,128)S(1)}, u32[]{:S(2)}, u32[]{:S(2)}) collective-permute-start(f32[256,256]{1,0:T(8,128)S(1)} %constant_dynamic-slice_fusion.2), channel_id=1, source_target_pairs={{0,8},{8,0},{16,24},{24,16},{1,9},{9,1},{17,25},{25,17},{2,10},{10... | collective-permute-start | bytes 786440 | tf_op jit(solution)/shard_map/ppermute | solution.py:30
  64.8 6.5 %collective-permute-start.9 = (f32[128,256]{1,0:T(8,128)S(1)}, f32[128,256]{1,0:T(8,128)S(1)}, u32[]{:S(2)}, u32[]{:S(2)}) collective-permute-start(f32[128,256]{1,0:T(8,128)S(1)} %constant_dynamic-slice_fusion.1), channel_id=1, source_target_pairs={{0,16},{8,24},{16,0},{24,8},{1,17},{9,25},{17,1},{25,9},{2,18},{10... | collective-permute-start | bytes 393224 | tf_op jit(solution)/shard_map/ppermute | solution.py:30
  71.3 4.7 %collective-permute-start.10 = (f32[64,256]{1,0:T(8,128)S(1)}, f32[64,256]{1,0:T(8,128)S(1)}, u32[]{:S(2)}, u32[]{:S(2)}) collective-permute-start(f32[64,256]{1,0:T(8,128)S(1)} %constant_dynamic-slice_fusion), channel_id=1, source_target_pairs={{0,1},{1,0},{2,3},{3,2},{4,5},{5,4},{6,7},{7,6},{8,9},{9,8},{10,11... | collective-permute-start | bytes 196616 | tf_op jit(solution)/shard_map/ppermute | solution.py:30
  76.1 4.3 %collective-permute-start.11 = (f32[64,256]{1,0:T(8,128)S(1)}, f32[64,256]{1,0:T(8,128)S(1)}, u32[]{:S(2)}, u32[]{:S(2)}) collective-permute-start(f32[64,256]{1,0:T(8,128)S(1)} %dynamic-slice_add_fusion.2), channel_id=1, source_target_pairs={{0,2},{1,3},{2,0},{3,1},{4,6},{5,7},{6,4},{7,5},{8,10},{9,11},{10,... | collective-permute-start | bytes 196616 | tf_op jit(solution)/shard_map/ppermute | solution.py:30
  80.4 5.2 %collective-permute-start.12 = (f32[64,256]{1,0:T(8,128)S(1)}, f32[64,256]{1,0:T(8,128)S(1)}, u32[]{:S(2)}, u32[]{:S(2)}) collective-permute-start(f32[64,256]{1,0:T(8,128)S(1)} %add.67), channel_id=1, source_target_pairs={{0,4},{1,5},{2,6},{3,7},{4,0},{5,1},{6,2},{7,3},{8,12},{9,13},{10,... | collective-permute-start | bytes 196616 | tf_op jit(solution)/shard_map/ppermute | solution.py:30
  85.7 4.4 %collective-permute-start.13 = (f32[64,256]{1,0:T(8,128)S(1)}, f32[64,256]{1,0:T(8,128)S(1)}, u32[]{:S(2)}, u32[]{:S(2)}) collective-permute-start(f32[64,256]{1,0:T(8,128)S(1)} %add.68), channel_id=1, source_target_pairs={{0,1},{1,0},{2,3},{3,2},{4,5},{5,4},{6,7},{7,6},{8,9},{9,8},{10,11... | collective-permute-start | bytes 196616 | tf_op jit(solution)/shard_map/ppermute | solution.py:30
  90.1 6.1 %collective-permute-start.14 = (f32[128,256]{1,0:T(8,128)S(1)}, f32[128,256]{1,0:T(8,128)S(1)}, u32[]{:S(2)}, u32[]{:S(2)}) collective-permute-start(f32[128,256]{1,0:T(8,128)S(1)} %pad_maximum_fusion.1), channel_id=1, source_target_pairs={{0,16},{8,24},{16,0},{24,8},{1,17},{9,25},{17,1},{25,9},{2,18},{10... | collective-permute-start | bytes 393224 | tf_op jit(solution)/shard_map/ppermute | solution.py:30
  91.9 9.7 %collective-permute-start.5 = (f32[2,256,256]{2,1,0:T(8,128)}, f32[2,256,256]{2,1,0:T(8,128)}, u32[]{:S(2)}, u32[]{:S(2)}) collective-permute-start(f32[2,256,256]{2,1,0:T(8,128)} %get-tuple-element.11), channel_id=1, source_target_pairs={{0,8},{8,16},{16,24},{1,9},{9,17},{17,25},{2,10},{10,18},{18,26},{... | collective-permute-start | bytes 1572872 | tf_op jit(solution)/shard_map/ppermute | solution.py:21
  94.0 30.2 %collective-permute-start.4 = (f32[2,256,512]{2,1,0:T(8,128)}, f32[2,256,512]{2,1,0:T(8,128)S(1)}, u32[]{:S(2)}, u32[]{:S(2)}) collective-permute-start(f32[2,256,512]{2,1,0:T(8,128)} %get-tuple-element.9), channel_id=1, source_target_pairs={{0,8},{8,16},{16,24},{1,9},{9,17},{17,25},{2,10},{10,18},{18,26},{... | collective-permute-start | bytes 3145736 | tf_op jit(solution)/shard_map/ppermute | solution.py:21
  96.2 28.1 %copy-start = (f32[2,512,512]{2,1,0:T(8,128)S(1)}, f32[2,512,512]{2,1,0:T(8,128)}, u32[]{:S(2)}) copy-start(f32[2,512,512]{2,1,0:T(8,128)} %get-tuple-element.8) | copy-start | bytes 6291460
  96.9 9.7 %collective-permute-start.15 = (f32[256,256]{1,0:T(8,128)}, f32[256,256]{1,0:T(8,128)}, u32[]{:S(2)}, u32[]{:S(2)}) collective-permute-start(f32[256,256]{1,0:T(8,128)} %pad_maximum_fusion), channel_id=1, source_target_pairs={{0,8},{8,0},{16,24},{24,16},{1,9},{9,1},{17,25},{25,17},{2,10},{10... | collective-permute-start | bytes 786440 | tf_op jit(solution)/shard_map/ppermute | solution.py:30
  96.9 16.5 %collective-permute-start.7 = (f32[2,256,256]{2,1,0:T(8,128)}, f32[2,256,256]{2,1,0:T(8,128)}, u32[]{:S(2)}, u32[]{:S(2)}) collective-permute-start(f32[2,256,256]{2,1,0:T(8,128)} %get-tuple-element.12), channel_id=1, source_target_pairs={{0,1},{1,2},{2,3},{3,4},{4,5},{5,6},{6,7},{8,9},{9,10},{10,11},{11... | collective-permute-start | bytes 1572872 | tf_op jit(solution)/shard_map/ppermute | solution.py:21
  103.7 20.5 %collective-permute-start.6 = (f32[2,256,256]{2,1,0:T(8,128)}, f32[2,256,256]{2,1,0:T(8,128)}, u32[]{:S(2)}, u32[]{:S(2)}) collective-permute-start(f32[2,256,256]{2,1,0:T(8,128)} %add.55), channel_id=1, source_target_pairs={{0,1},{1,2},{2,3},{3,4},{4,5},{5,6},{6,7},{8,9},{9,10},{10,11},{11... | collective-permute-start | bytes 1572872 | tf_op jit(solution)/shard_map/ppermute | solution.py:21

commit v3 on v2

--- a/solution.py
+++ b/solution.py
@@ -30,14 +30,18 @@
     return lax.ppermute(value, axis, [(at, at ^ bit) for at in range(lax.axis_size(axis))])
 
 
-def summed_over(value, axes):
+def summed_over(value, axes, corner, low, later):
     if any(lax.axis_size(axis) & (lax.axis_size(axis) - 1) for axis in axes):
-        return lax.psum(value, axes)
+        return lax.psum(value, axes), (low, *later(corner))
     rounds = [pair for axis in axes for pair in bit_partners(axis)]
     shape = value.shape
     value = value.reshape(-1, shape[-1])
     split = []
-    for axis, bit in rounds:
+    for number, (axis, bit) in enumerate(rounds):
+        if number == 1:
+            value, corner = lax.optimization_barrier((value, corner))
+        if number == 4:
+            value, low = lax.optimization_barrier((value, low))
         half = value.shape[0] // 2
         if len(split) < 3 and half % SUBLANES == 0:
             upper = (lax.axis_index(axis) & bit) // bit
@@ -47,12 +51,15 @@
             split.append((axis, bit, upper))
         else:
             value = value + swapped(value, axis, bit)
-    for axis, bit, upper in reversed(split):
+    beside = (low, *later(corner))
+    for number, (axis, bit, upper) in enumerate(reversed(split)):
+        if number == 1:
+            value, beside = lax.optimization_barrier((value, beside))
         other = swapped(value, axis, bit)
         first = jnp.where(upper == 0, value, other)
         second = jnp.where(upper == 0, other, value)
         value = jnp.concatenate([first, second], axis=0)
-    return value.reshape(shape)
+    return value.reshape(shape), beside
 
 
 def halves_np(table):
@@ -227,14 +234,17 @@
     )
     got_corner = passed_along(g_corner, "row", 1)
     got_low = passed_along(g_low, "col", 1)
-    got_rows = passed_along(g_below, "row", 1)
-    got_top = passed_along(g_top + got_corner, "col", 1)
+    later = lambda corner: (
+        passed_along(g_below, "row", 1), passed_along(g_top + corner, "col", 1)
+    )
+    probe_total, (got_low, got_rows, got_top) = summed_over(
+        probe_acc, ("row", "col"), got_corner, got_low, later
+    )
     pad = lambda value, top: jnp.pad(
         value, ((0, 0), (top, rows - top - value.shape[1]), (0, cols - value.shape[2]))
     )
     object_grad = g_main + pad(got_rows, 0) + pad(got_top, 0) + pad(got_low, side)
     count = positions * lax.axis_size("row") * lax.axis_size("col")
-    probe_total = summed_over(probe_acc, ("row", "col"))
     return (object_grad, probe_total / count)
 
 

time: 128 us -> 126 us (0.984)
  the two profiles are of different devices: /device:TPU:0 before, /device:TPU:31 now
where the time goes in v3:
time: 126 us; the launch traced here: 125 us
  waiting for transfers between devices  47.7 us (38%)
  starting transfers between devices  36.7 us (29%)
  Pallas kernels  28.1 us (22%)
  other arithmetic  7.86 us (6%)
  local copies, waits for them, and re-layouts  4.21 us (3%)
    ppermute x8, waiting for transfers between devices, swapped(): lax.ppermute(value, axis, [(at, at ^ bit) for at in range(lax.axis_size(a...  33.3 us
    pallas_call x1, Pallas kernels, all_positions(): pl.pallas_call(functools.partial(kernel, (side, rows, cols)), grid=(count...  28.1 us
    ppermute x8, starting transfers between devices, swapped(): lax.ppermute(value, axis, [(at, at ^ bit) for at in range(lax.axis_size(a...  19 us
    ppermute x8, starting transfers between devices, passed_along(): lax.ppermute(value, axis, [(source, source + steps) for source in range(f...  17.6 us
    ppermute x8, waiting for transfers between devices, passed_along(): lax.ppermute(value, axis, [(source, source + steps) for source in range(f...  14.4 us
    add x1, other arithmetic, shards(): g_main + pad(got_rows, 0) + pad(got_top, 0) + pad(got_low, side)  2.93 us
  transfers between devices with their start and end apart: 16, of which 7 were waited for; matrix products, arithmetic and copies ran while one was open for 7% of the time, Pallas kernels for 0%

profile of v3, /device:TPU:31, one launch (start us, length us, event | category | flops | bytes accessed | tf_op | source)
XLA Modules:
  0.0 125.5 jit_solution(1168515079144975434)
XLA Ops:
  0.7 1.4 %slice.9 = f32[2,256,512]{2,1,0:T(8,128)S(1)} slice(f32[2,512,512]{2,1,0:T(8,128)} %obj.1), slice={[0:2], [0:256], [0:512]} | slice | bytes 2097152 | tf_op jit(solution)/shard_map/slice | solution.py:229
  2.1 2.6 %collective-permute-start = (f32[2,256,512]{2,1,0:T(8,128)S(1)}, f32[2,256,512]{2,1,0:T(8,128)S(1)}, u32[]{:S(2)}, u32[]{:S(2)}) collective-permute-start(f32[2,256,512]{2,1,0:T(8,128)S(1)} %slice.9), channel_id=1, source_target_pairs={{8,0},{16,8},{24,16},{9,1},{17,9},{25,17},{10,2},{18,10},{26,18},{... | collective-permute-start | bytes 3145736 | tf_op jit(solution)/shard_map/ppermute | solution.py:21
  4.9 2.2 %collective-permute-start.1 = (f32[2,256,256]{2,1,0:T(8,128)S(1)}, f32[2,256,256]{2,1,0:T(8,128)S(1)}, u32[]{:S(2)}, u32[]{:S(2)}) collective-permute-start(f32[2,256,256]{2,1,0:T(8,128)S(1)} %get-tuple-element.31), channel_id=1, source_target_pairs={{1,0},{2,1},{3,2},{4,3},{5,4},{6,5},{7,6},{9,8},{10,9},{11,10},{12... | collective-permute-start | bytes 1572872 | tf_op jit(solution)/shard_map/ppermute | solution.py:21
  7.0 3.8 %collective-permute-start.2 = (f32[2,256,256]{2,1,0:T(8,128)S(1)}, f32[2,256,256]{2,1,0:T(8,128)}, u32[]{:S(2)}, u32[]{:S(2)}) collective-permute-start(f32[2,256,256]{2,1,0:T(8,128)S(1)} %get-tuple-element.30), channel_id=1, source_target_pairs={{1,0},{2,1},{3,2},{4,3},{5,4},{6,5},{7,6},{9,8},{10,9},{11,10},{12... | collective-permute-start | bytes 1572872 | tf_op jit(solution)/shard_map/ppermute | solution.py:21
  10.9 7.6 %collective-permute-done.1.right_top = f32[2,256,256]{2,1,0:T(8,128)S(1)} collective-permute-done((f32[2,256,256]{2,1,0:T(8,128)S(1)}, f32[2,256,256]{2,1,0:T(8,128)S(1)}, u32[]{:S(2)}, u32[]{:S(2)}) %collective-permute-start.1) | collective-permute-done | bytes 524320 | tf_op jit(solution)/shard_map/ppermute | solution.py:21
  18.4 3.7 %collective-permute-start.3 = (f32[2,256,256]{2,1,0:T(8,128)S(1)}, f32[2,256,256]{2,1,0:T(8,128)}, u32[]{:S(2)}, u32[]{:S(2)}) collective-permute-start(f32[2,256,256]{2,1,0:T(8,128)S(1)} %collective-permute-done.1.right_top), channel_id=1, source_target_pairs={{8,0},{16,8},{24,16},{9,1},{17,9},{25,17},{10,2},{18,10},{26,18},{... | collective-permute-start | bytes 1572872 | tf_op jit(solution)/shard_map/ppermute | solution.py:21
  22.1 0.7 copy.8.off
  22.8 6.8 %collective-permute-done.2.right_low = f32[2,256,256]{2,1,0:T(8,128)} collective-permute-done((f32[2,256,256]{2,1,0:T(8,128)S(1)}, f32[2,256,256]{2,1,0:T(8,128)}, u32[]{:S(2)}, u32[]{:S(2)}) %collective-permute-start.2) | collective-permute-done | bytes 524320 | tf_op jit(solution)/shard_map/ppermute | solution.py:21
  29.7 1.0 copy-done.4
  30.6 28.1 %shard_map.77 = (f32[2,512,512]{2,1,0:T(8,128)}, f32[2,256,512]{2,1,0:T(8,128)}, f32[2,256,256]{2,1,0:T(8,128)}, f32[2,256,256]{2,1,0:T(8,128)}, f32[2,256,256]{2,1,0:T(8,128)}, /*index=5*/f32[2,256,256]{2,1,0:T(8,128)}) custom-call(s32[1,1,8,2]{3,2,1,0:T(8,128)} %copy.8.off, f32[2,512,512]{2,1,0:T(8,128)} %obj.1, f32[2,256,512]{2,1,0:T(8,128)} %copy-done.4, ...), custom_call_target="tpu_custom_call" | custom-call | flops 9663676416 | bytes 12582912 | tf_op jit(solution)/shard_map/pallas_call | solution.py:192
  58.8 1.3 %collective-permute-start.5 = (f32[2,256,256]{2,1,0:T(8,128)}, f32[2,256,256]{2,1,0:T(8,128)S(1)}, u32[]{:S(2)}, u32[]{:S(2)}) collective-permute-start(f32[2,256,256]{2,1,0:T(8,128)} %get-tuple-element.18), channel_id=1, source_target_pairs={{0,8},{8,16},{16,24},{1,9},{9,17},{17,25},{2,10},{10,18},{18,26},{... | collective-permute-start | bytes 1572872 | tf_op jit(solution)/shard_map/ppermute | solution.py:21
  60.1 1.0 constant_dynamic-slice_fusion.2
  61.0 1.5 %collective-permute-start.4 = (f32[256,256]{1,0:T(8,128)S(1)}, f32[256,256]{1,0:T(8,128)S(1)}, u32[]{:S(2)}, u32[]{:S(2)}) collective-permute-start(f32[256,256]{1,0:T(8,128)S(1)} %constant_dynamic-slice_fusion.2), channel_id=1, source_target_pairs={{0,8},{8,0},{16,24},{24,16},{1,9},{9,1},{17,25},{25,17},{2,10},{10... | collective-permute-start | bytes 786440 | tf_op jit(solution)/shard_map/ppermute | solution.py:30
  62.5 1.2 collective-permute-done.4
  63.7 1.0 dynamic-slice_add_fusion
  64.7 4.6 %collective-permute-start.6 = (f32[128,256]{1,0:T(8,128)S(1)}, f32[128,256]{1,0:T(8,128)}, u32[]{:S(2)}, u32[]{:S(2)}) collective-permute-start(f32[128,256]{1,0:T(8,128)S(1)} %constant_dynamic-slice_fusion.1), channel_id=1, source_target_pairs={{0,16},{8,24},{16,0},{24,8},{1,17},{9,25},{17,1},{25,9},{2,18},{10... | collective-permute-start | bytes 393224 | tf_op jit(solution)/shard_map/ppermute | solution.py:30
  69.3 1.3 %collective-permute-start.9 = (f32[2,256,256]{2,1,0:T(8,128)}, f32[2,256,256]{2,1,0:T(8,128)}, u32[]{:S(2)}, u32[]{:S(2)}) collective-permute-start(f32[2,256,256]{2,1,0:T(8,128)} %get-tuple-element.20), channel_id=1, source_target_pairs={{0,1},{1,2},{2,3},{3,4},{4,5},{5,6},{6,7},{8,9},{9,10},{10,11},{11... | collective-permute-start | bytes 1572872 | tf_op jit(solution)/shard_map/ppermute | solution.py:21
  70.6 1.4 %collective-permute-start.12 = (f32[2,256,512]{2,1,0:T(8,128)}, f32[2,256,512]{2,1,0:T(8,128)S(1)}, u32[]{:S(2)}, u32[]{:S(2)}) collective-permute-start(f32[2,256,512]{2,1,0:T(8,128)} %get-tuple-element.23), channel_id=1, source_target_pairs={{0,8},{8,16},{16,24},{1,9},{9,17},{17,25},{2,10},{10,18},{18,26},{... | collective-permute-start | bytes 3145736 | tf_op jit(solution)/shard_map/ppermute | solution.py:21
  72.1 0.9 dynamic-slice_add_fusion.1
  73.0 3.0 %collective-permute-start.7 = (f32[64,256]{1,0:T(8,128)S(1)}, f32[64,256]{1,0:T(8,128)S(1)}, u32[]{:S(2)}, u32[]{:S(2)}) collective-permute-start(f32[64,256]{1,0:T(8,128)S(1)} %constant_dynamic-slice_fusion), channel_id=1, source_target_pairs={{0,1},{1,0},{2,3},{3,2},{4,5},{5,4},{6,7},{7,6},{8,9},{9,8},{10,11... | collective-permute-start | bytes 196616 | tf_op jit(solution)/shard_map/ppermute | solution.py:30
  76.0 11.6 %collective-permute-done.7 = f32[64,256]{1,0:T(8,128)S(1)} collective-permute-done((f32[64,256]{1,0:T(8,128)S(1)}, f32[64,256]{1,0:T(8,128)S(1)}, u32[]{:S(2)}, u32[]{:S(2)}) %collective-permute-start.7) | collective-permute-done | bytes 65568 | tf_op jit(solution)/shard_map/ppermute | solution.py:30
  87.7 0.8 collective-permute-start.8
  88.5 2.1 %add.65 = f32[2,256,256]{2,1,0:T(8,128)} add(f32[2,256,256]{2,1,0:T(8,128)} %get-tuple-element.24, f32[2,256,256]{2,1,0:T(8,128)} %copy-done.2) | non-fusion elementwise | flops 131072 | bytes 1572864 | tf_op jit(solution)/shard_map/add | solution.py:238
  90.6 1.3 %collective-permute-start.13 = (f32[2,256,256]{2,1,0:T(8,128)}, f32[2,256,256]{2,1,0:T(8,128)}, u32[]{:S(2)}, u32[]{:S(2)}) collective-permute-start(f32[2,256,256]{2,1,0:T(8,128)} %add.65), channel_id=1, source_target_pairs={{0,1},{1,2},{2,3},{3,4},{4,5},{5,6},{6,7},{8,9},{9,10},{10,11},{11... | collective-permute-start | bytes 1572872 | tf_op jit(solution)/shard_map/ppermute | solution.py:21
  91.9 4.5 %collective-permute-start.10 = (f32[64,256]{1,0:T(8,128)S(1)}, f32[64,256]{1,0:T(8,128)S(1)}, u32[]{:S(2)}, u32[]{:S(2)}) collective-permute-start(f32[64,256]{1,0:T(8,128)S(1)} %add.63), channel_id=1, source_target_pairs={{0,4},{1,5},{2,6},{3,7},{4,0},{5,1},{6,2},{7,3},{8,12},{9,13},{10,... | collective-permute-start | bytes 196616 | tf_op jit(solution)/shard_map/ppermute | solution.py:30
  96.4 13.8 %collective-permute-done.10 = f32[64,256]{1,0:T(8,128)S(1)} collective-permute-done((f32[64,256]{1,0:T(8,128)S(1)}, f32[64,256]{1,0:T(8,128)S(1)}, u32[]{:S(2)}, u32[]{:S(2)}) %collective-permute-start.10) | collective-permute-done | bytes 65568 | tf_op jit(solution)/shard_map/ppermute | solution.py:30
  110.3 3.1 %collective-permute-done.11 = f32[64,256]{1,0:T(8,128)S(1)} collective-permute-done((f32[64,256]{1,0:T(8,128)S(1)}, f32[64,256]{1,0:T(8,128)S(1)}, u32[]{:S(2)}, u32[]{:S(2)}) %collective-permute-start.11) | collective-permute-done | bytes 65568 | tf_op jit(solution)/shard_map/ppermute | solution.py:30
  113.4 0.3 collective-permute-start.14
  113.7 3.6 %collective-permute-done.14 = f32[128,256]{1,0:T(8,128)S(1)} collective-permute-done((f32[128,256]{1,0:T(8,128)S(1)}, f32[128,256]{1,0:T(8,128)S(1)}, u32[]{:S(2)}, u32[]{:S(2)}) %collective-permute-start.14) | collective-permute-done | bytes 131104 | tf_op jit(solution)/shard_map/ppermute | solution.py:30
  117.4 4.3 %collective-permute-start.15 = (f32[256,256]{1,0:T(8,128)S(1)}, f32[256,256]{1,0:T(8,128)S(1)}, u32[]{:S(2)}, u32[]{:S(2)}) collective-permute-start(f32[256,256]{1,0:T(8,128)S(1)} %pad_maximum_fusion), channel_id=1, source_target_pairs={{0,8},{8,0},{16,24},{24,16},{1,9},{9,1},{17,25},{25,17},{2,10},{10... | collective-permute-start | bytes 786440 | tf_op jit(solution)/shard_map/ppermute | solution.py:30
  121.7 2.9 %pad_add_fusion = f32[2,512,512]{2,1,0:T(8,128)} fusion(f32[2,256,256]{2,1,0:T(8,128)} %collective-permute-done.9, f32[2,256,256]{2,1,0:T(8,128)} %collective-permute-done.13, f32[2,512,512]{2,1,0:T(8,128)S(1)} %copy-done, f32[2,256,512]{2,1,0:T(8,128)S(1)} %collective-permute-done.12), kind=kLoop, calls=%fused_computation | loop fusion | flops 1572864 | bytes 6291456 | tf_op jit(solution)/shard_map/add | solution.py:246
  124.7 0.8 maximum_multiply_fusion
  (32 shorter events, 0.4 us)
Async XLA Ops:
  0.6 4.1 %copy-start.1 = (f32[2,512,512]{2,1,0:T(8,128)S(1)}, f32[2,512,512]{2,1,0:T(8,128)}, u32[]{:S(2)}) copy-start(f32[2,512,512]{2,1,0:T(8,128)} %obj.1) | copy-start | bytes 6291460
  0.6 21.5 %copy-start.3 = (s32[1,1,8,2]{2,3,1,0:T(2,128)S(1)}, s32[1,1,8,2]{2,3,1,0:T(2,128)}, u32[]{:S(2)}) copy-start(s32[1,1,8,2]{2,3,1,0:T(2,128)} %param.9) | copy-start | bytes 196
  2.1 27.6 %collective-permute-start = (f32[2,256,512]{2,1,0:T(8,128)S(1)}, f32[2,256,512]{2,1,0:T(8,128)S(1)}, u32[]{:S(2)}, u32[]{:S(2)}) collective-permute-start(f32[2,256,512]{2,1,0:T(8,128)S(1)} %slice.9), channel_id=1, source_target_pairs={{8,0},{16,8},{24,16},{9,1},{17,9},{25,17},{10,2},{18,10},{26,18},{... | collective-permute-start | bytes 3145736 | tf_op jit(solution)/shard_map/ppermute | solution.py:21
  4.9 13.5 %collective-permute-start.1 = (f32[2,256,256]{2,1,0:T(8,128)S(1)}, f32[2,256,256]{2,1,0:T(8,128)S(1)}, u32[]{:S(2)}, u32[]{:S(2)}) collective-permute-start(f32[2,256,256]{2,1,0:T(8,128)S(1)} %get-tuple-element.31), channel_id=1, source_target_pairs={{1,0},{2,1},{3,2},{4,3},{5,4},{6,5},{7,6},{9,8},{10,9},{11,10},{12... | collective-permute-start | bytes 1572872 | tf_op jit(solution)/shard_map/ppermute | solution.py:21
  7.0 22.6 %collective-permute-start.2 = (f32[2,256,256]{2,1,0:T(8,128)S(1)}, f32[2,256,256]{2,1,0:T(8,128)}, u32[]{:S(2)}, u32[]{:S(2)}) collective-permute-start(f32[2,256,256]{2,1,0:T(8,128)S(1)} %get-tuple-element.30), channel_id=1, source_target_pairs={{1,0},{2,1},{3,2},{4,3},{5,4},{6,5},{7,6},{9,8},{10,9},{11,10},{12... | collective-permute-start | bytes 1572872 | tf_op jit(solution)/shard_map/ppermute | solution.py:21
  18.4 11.2 %copy-start.5 = (f32[2,256,256]{2,1,0:T(8,128)}, f32[2,256,256]{2,1,0:T(8,128)S(1)}, u32[]{:S(2)}) copy-start(f32[2,256,256]{2,1,0:T(8,128)S(1)} %collective-permute-done.1.right_top) | copy-start | bytes 1572868
  18.4 11.2 %collective-permute-start.3 = (f32[2,256,256]{2,1,0:T(8,128)S(1)}, f32[2,256,256]{2,1,0:T(8,128)}, u32[]{:S(2)}, u32[]{:S(2)}) collective-permute-start(f32[2,256,256]{2,1,0:T(8,128)S(1)} %collective-permute-done.1.right_top), channel_id=1, source_target_pairs={{8,0},{16,8},{24,16},{9,1},{17,9},{25,17},{10,2},{18,10},{26,18},{... | collective-permute-start | bytes 1572872 | tf_op jit(solution)/shard_map/ppermute | solution.py:21
  29.7 1.0 copy-start.4
  58.8 5.9 %collective-permute-start.5 = (f32[2,256,256]{2,1,0:T(8,128)}, f32[2,256,256]{2,1,0:T(8,128)S(1)}, u32[]{:S(2)}, u32[]{:S(2)}) collective-permute-start(f32[2,256,256]{2,1,0:T(8,128)} %get-tuple-element.18), channel_id=1, source_target_pairs={{0,8},{8,16},{16,24},{1,9},{9,17},{17,25},{2,10},{10,18},{18,26},{... | collective-permute-start | bytes 1572872 | tf_op jit(solution)/shard_map/ppermute | solution.py:21
  61.0 2.7 %collective-permute-start.4 = (f32[256,256]{1,0:T(8,128)S(1)}, f32[256,256]{1,0:T(8,128)S(1)}, u32[]{:S(2)}, u32[]{:S(2)}) collective-permute-start(f32[256,256]{1,0:T(8,128)S(1)} %constant_dynamic-slice_fusion.2), channel_id=1, source_target_pairs={{0,8},{8,0},{16,24},{24,16},{1,9},{9,1},{17,25},{25,17},{2,10},{10... | collective-permute-start | bytes 786440 | tf_op jit(solution)/shard_map/ppermute | solution.py:30
  64.7 5.9 %copy-start.2 = (f32[2,256,256]{2,1,0:T(8,128)}, f32[2,256,256]{2,1,0:T(8,128)S(1)}, u32[]{:S(2)}) copy-start(f32[2,256,256]{2,1,0:T(8,128)S(1)} %collective-permute-done.5) | copy-start | bytes 1572868
  64.7 7.3 %collective-permute-start.6 = (f32[128,256]{1,0:T(8,128)S(1)}, f32[128,256]{1,0:T(8,128)}, u32[]{:S(2)}, u32[]{:S(2)}) collective-permute-start(f32[128,256]{1,0:T(8,128)S(1)} %constant_dynamic-slice_fusion.1), channel_id=1, source_target_pairs={{0,16},{8,24},{16,0},{24,8},{1,17},{9,25},{17,1},{25,9},{2,18},{10... | collective-permute-start | bytes 393224 | tf_op jit(solution)/shard_map/ppermute | solution.py:30
  69.3 22.6 %collective-permute-start.9 = (f32[2,256,256]{2,1,0:T(8,128)}, f32[2,256,256]{2,1,0:T(8,128)}, u32[]{:S(2)}, u32[]{:S(2)}) collective-permute-start(f32[2,256,256]{2,1,0:T(8,128)} %get-tuple-element.20), channel_id=1, source_target_pairs={{0,1},{1,2},{2,3},{3,4},{4,5},{5,6},{6,7},{8,9},{9,10},{10,11},{11... | collective-permute-start | bytes 1572872 | tf_op jit(solution)/shard_map/ppermute | solution.py:21
  70.6 51.1 %copy-start = (f32[2,512,512]{2,1,0:T(8,128)S(1)}, f32[2,512,512]{2,1,0:T(8,128)}, u32[]{:S(2)}) copy-start(f32[2,512,512]{2,1,0:T(8,128)} %get-tuple-element.16) | copy-start | bytes 6291460
  70.6 42.8 %collective-permute-start.12 = (f32[2,256,512]{2,1,0:T(8,128)}, f32[2,256,512]{2,1,0:T(8,128)S(1)}, u32[]{:S(2)}, u32[]{:S(2)}) collective-permute-start(f32[2,256,512]{2,1,0:T(8,128)} %get-tuple-element.23), channel_id=1, source_target_pairs={{0,8},{8,16},{16,24},{1,9},{9,17},{17,25},{2,10},{10,18},{18,26},{... | collective-permute-start | bytes 3145736 | tf_op jit(solution)/shard_map/ppermute | solution.py:21
  73.0 14.6 %collective-permute-start.7 = (f32[64,256]{1,0:T(8,128)S(1)}, f32[64,256]{1,0:T(8,128)S(1)}, u32[]{:S(2)}, u32[]{:S(2)}) collective-permute-start(f32[64,256]{1,0:T(8,128)S(1)} %constant_dynamic-slice_fusion), channel_id=1, source_target_pairs={{0,1},{1,0},{2,3},{3,2},{4,5},{5,4},{6,7},{7,6},{8,9},{9,8},{10,11... | collective-permute-start | bytes 196616 | tf_op jit(solution)/shard_map/ppermute | solution.py:30
  87.7 4.2 %collective-permute-start.8 = (f32[64,256]{1,0:T(8,128)S(1)}, f32[64,256]{1,0:T(8,128)S(1)}, u32[]{:S(2)}, u32[]{:S(2)}) collective-permute-start(f32[64,256]{1,0:T(8,128)S(1)} %dynamic-slice_add_fusion.2), channel_id=1, source_target_pairs={{0,2},{1,3},{2,0},{3,1},{4,6},{5,7},{6,4},{7,5},{8,10},{9,11},{10,... | collective-permute-start | bytes 196616 | tf_op jit(solution)/shard_map/ppermute | solution.py:30
  90.6 22.8 %collective-permute-start.13 = (f32[2,256,256]{2,1,0:T(8,128)}, f32[2,256,256]{2,1,0:T(8,128)}, u32[]{:S(2)}, u32[]{:S(2)}) collective-permute-start(f32[2,256,256]{2,1,0:T(8,128)} %add.65), channel_id=1, source_target_pairs={{0,1},{1,2},{2,3},{3,4},{4,5},{5,6},{6,7},{8,9},{9,10},{10,11},{11... | collective-permute-start | bytes 1572872 | tf_op jit(solution)/shard_map/ppermute | solution.py:21
  91.9 18.3 %collective-permute-start.10 = (f32[64,256]{1,0:T(8,128)S(1)}, f32[64,256]{1,0:T(8,128)S(1)}, u32[]{:S(2)}, u32[]{:S(2)}) collective-permute-start(f32[64,256]{1,0:T(8,128)S(1)} %add.63), channel_id=1, source_target_pairs={{0,4},{1,5},{2,6},{3,7},{4,0},{5,1},{6,2},{7,3},{8,12},{9,13},{10,... | collective-permute-start | bytes 196616 | tf_op jit(solution)/shard_map/ppermute | solution.py:30
  110.2 3.2 %collective-permute-start.11 = (f32[64,256]{1,0:T(8,128)S(1)}, f32[64,256]{1,0:T(8,128)S(1)}, u32[]{:S(2)}, u32[]{:S(2)}) collective-permute-start(f32[64,256]{1,0:T(8,128)S(1)} %add.64), channel_id=1, source_target_pairs={{0,1},{1,0},{2,3},{3,2},{4,5},{5,4},{6,7},{7,6},{8,9},{9,8},{10,11... | collective-permute-start | bytes 196616 | tf_op jit(solution)/shard_map/ppermute | solution.py:30
  113.4 3.9 %collective-permute-start.14 = (f32[128,256]{1,0:T(8,128)S(1)}, f32[128,256]{1,0:T(8,128)S(1)}, u32[]{:S(2)}, u32[]{:S(2)}) collective-permute-start(f32[128,256]{1,0:T(8,128)S(1)} %pad_maximum_fusion.1), channel_id=1, source_target_pairs={{0,16},{8,24},{16,0},{24,8},{1,17},{9,25},{17,1},{25,9},{2,18},{10... | collective-permute-start | bytes 393224 | tf_op jit(solution)/shard_map/ppermute | solution.py:30
  117.4 7.3 %collective-permute-start.15 = (f32[256,256]{1,0:T(8,128)S(1)}, f32[256,256]{1,0:T(8,128)S(1)}, u32[]{:S(2)}, u32[]{:S(2)}) collective-permute-start(f32[256,256]{1,0:T(8,128)S(1)} %pad_maximum_fusion), channel_id=1, source_target_pairs={{0,8},{8,0},{16,24},{24,16},{1,9},{9,1},{17,25},{25,17},{2,10},{10... | collective-permute-start | bytes 786440 | tf_op jit(solution)/shard_map/ppermute | solution.py:30

commit v4 on v3

--- a/solution.py
+++ b/solution.py
@@ -12,7 +12,7 @@
 
 LANES = 128
 SUBLANES = 8
-GROUP = 2
+GROUP = 4
 
 
 def passed_along(value, axis, steps):

time: 126 us -> 125 us (level)
  no operation moved by 1% of the time
where the time goes in v4:
time: 125 us
  waiting for transfers between devices  47.7 us (38%)
  starting transfers between devices  36.7 us (29%)
  Pallas kernels  27.2 us (22%)
  other arithmetic  7.86 us (6%)
  local copies, waits for them, and re-layouts  4.21 us (3%)
    ppermute x8, waiting for transfers between devices, swapped(): lax.ppermute(value, axis, [(at, at ^ bit) for at in range(lax.axis_size(a...  33.3 us
    pallas_call x1, Pallas kernels, all_positions(): pl.pallas_call(functools.partial(kernel, (side, rows, cols)), grid=(count...  27.2 us
    ppermute x8, starting transfers between devices, swapped(): lax.ppermute(value, axis, [(at, at ^ bit) for at in range(lax.axis_size(a...  19.1 us
    ppermute x8, starting transfers between devices, passed_along(): lax.ppermute(value, axis, [(source, source + steps) for source in range(f...  17.6 us
    ppermute x8, waiting for transfers between devices, passed_along(): lax.ppermute(value, axis, [(source, source + steps) for source in range(f...  14.4 us
    add x1, other arithmetic, shards(): g_main + pad(got_rows, 0) + pad(got_top, 0) + pad(got_low, side)  2.93 us
  transfers between devices with their start and end apart: 16, of which 7 were waited for; matrix products, arithmetic and copies ran while one was open for 7% of the time, Pallas kernels for 0%

profile of v4, /device:TPU:31, one launch (start us, length us, event | category | flops | bytes accessed | tf_op | source)
XLA Modules:
  0.0 124.5 jit_solution(13946571464533857690)
XLA Ops:
  0.7 1.4 %slice.9 = f32[2,256,512]{2,1,0:T(8,128)S(1)} slice(f32[2,512,512]{2,1,0:T(8,128)} %obj.1), slice={[0:2], [0:256], [0:512]} | slice | bytes 2097152 | tf_op jit(solution)/shard_map/slice | solution.py:229
  2.1 2.6 %collective-permute-start = (f32[2,256,512]{2,1,0:T(8,128)S(1)}, f32[2,256,512]{2,1,0:T(8,128)S(1)}, u32[]{:S(2)}, u32[]{:S(2)}) collective-permute-start(f32[2,256,512]{2,1,0:T(8,128)S(1)} %slice.9), channel_id=1, source_target_pairs={{8,0},{16,8},{24,16},{9,1},{17,9},{25,17},{10,2},{18,10},{26,18},{... | collective-permute-start | bytes 3145736 | tf_op jit(solution)/shard_map/ppermute | solution.py:21
  4.9 2.2 %collective-permute-start.1 = (f32[2,256,256]{2,1,0:T(8,128)S(1)}, f32[2,256,256]{2,1,0:T(8,128)S(1)}, u32[]{:S(2)}, u32[]{:S(2)}) collective-permute-start(f32[2,256,256]{2,1,0:T(8,128)S(1)} %get-tuple-element.31), channel_id=1, source_target_pairs={{1,0},{2,1},{3,2},{4,3},{5,4},{6,5},{7,6},{9,8},{10,9},{11,10},{12... | collective-permute-start | bytes 1572872 | tf_op jit(solution)/shard_map/ppermute | solution.py:21
  7.0 3.8 %collective-permute-start.2 = (f32[2,256,256]{2,1,0:T(8,128)S(1)}, f32[2,256,256]{2,1,0:T(8,128)}, u32[]{:S(2)}, u32[]{:S(2)}) collective-permute-start(f32[2,256,256]{2,1,0:T(8,128)S(1)} %get-tuple-element.30), channel_id=1, source_target_pairs={{1,0},{2,1},{3,2},{4,3},{5,4},{6,5},{7,6},{9,8},{10,9},{11,10},{12... | collective-permute-start | bytes 1572872 | tf_op jit(solution)/shard_map/ppermute | solution.py:21
  10.9 7.6 %collective-permute-done.1.right_top = f32[2,256,256]{2,1,0:T(8,128)S(1)} collective-permute-done((f32[2,256,256]{2,1,0:T(8,128)S(1)}, f32[2,256,256]{2,1,0:T(8,128)S(1)}, u32[]{:S(2)}, u32[]{:S(2)}) %collective-permute-start.1) | collective-permute-done | bytes 524320 | tf_op jit(solution)/shard_map/ppermute | solution.py:21
  18.4 3.7 %collective-permute-start.3 = (f32[2,256,256]{2,1,0:T(8,128)S(1)}, f32[2,256,256]{2,1,0:T(8,128)}, u32[]{:S(2)}, u32[]{:S(2)}) collective-permute-start(f32[2,256,256]{2,1,0:T(8,128)S(1)} %collective-permute-done.1.right_top), channel_id=1, source_target_pairs={{8,0},{16,8},{24,16},{9,1},{17,9},{25,17},{10,2},{18,10},{26,18},{... | collective-permute-start | bytes 1572872 | tf_op jit(solution)/shard_map/ppermute | solution.py:21
  22.1 0.7 copy.8.off
  22.8 6.8 %collective-permute-done.2.right_low = f32[2,256,256]{2,1,0:T(8,128)} collective-permute-done((f32[2,256,256]{2,1,0:T(8,128)S(1)}, f32[2,256,256]{2,1,0:T(8,128)}, u32[]{:S(2)}, u32[]{:S(2)}) %collective-permute-start.2) | collective-permute-done | bytes 524320 | tf_op jit(solution)/shard_map/ppermute | solution.py:21
  29.7 1.0 copy-done.4
  30.6 27.2 %shard_map.77 = (f32[2,512,512]{2,1,0:T(8,128)}, f32[2,256,512]{2,1,0:T(8,128)}, f32[2,256,256]{2,1,0:T(8,128)}, f32[2,256,256]{2,1,0:T(8,128)}, f32[2,256,256]{2,1,0:T(8,128)}, /*index=5*/f32[2,256,256]{2,1,0:T(8,128)}) custom-call(s32[1,1,8,2]{3,2,1,0:T(8,128)} %copy.8.off, f32[2,512,512]{2,1,0:T(8,128)} %obj.1, f32[2,256,512]{2,1,0:T(8,128)} %copy-done.4, ...), custom_call_target="tpu_custom_call" | custom-call | flops 9663676416 | bytes 12582912 | tf_op jit(solution)/shard_map/pallas_call | solution.py:192
  57.8 1.3 %collective-permute-start.5 = (f32[2,256,256]{2,1,0:T(8,128)}, f32[2,256,256]{2,1,0:T(8,128)S(1)}, u32[]{:S(2)}, u32[]{:S(2)}) collective-permute-start(f32[2,256,256]{2,1,0:T(8,128)} %get-tuple-element.18), channel_id=1, source_target_pairs={{0,8},{8,16},{16,24},{1,9},{9,17},{17,25},{2,10},{10,18},{18,26},{... | collective-permute-start | bytes 1572872 | tf_op jit(solution)/shard_map/ppermute | solution.py:21
  59.1 1.0 constant_dynamic-slice_fusion.2
  60.1 1.4 %collective-permute-start.4 = (f32[256,256]{1,0:T(8,128)S(1)}, f32[256,256]{1,0:T(8,128)S(1)}, u32[]{:S(2)}, u32[]{:S(2)}) collective-permute-start(f32[256,256]{1,0:T(8,128)S(1)} %constant_dynamic-slice_fusion.2), channel_id=1, source_target_pairs={{0,8},{8,0},{16,24},{24,16},{1,9},{9,1},{17,25},{25,17},{2,10},{10... | collective-permute-start | bytes 786440 | tf_op jit(solution)/shard_map/ppermute | solution.py:30
  61.4 1.2 collective-permute-done.4
  62.6 1.0 dynamic-slice_add_fusion
  63.6 4.6 %collective-permute-start.6 = (f32[128,256]{1,0:T(8,128)S(1)}, f32[128,256]{1,0:T(8,128)}, u32[]{:S(2)}, u32[]{:S(2)}) collective-permute-start(f32[128,256]{1,0:T(8,128)S(1)} %constant_dynamic-slice_fusion.1), channel_id=1, source_target_pairs={{0,16},{8,24},{16,0},{24,8},{1,17},{9,25},{17,1},{25,9},{2,18},{10... | collective-permute-start | bytes 393224 | tf_op jit(solution)/shard_map/ppermute | solution.py:30
  68.2 1.3 %collective-permute-start.9 = (f32[2,256,256]{2,1,0:T(8,128)}, f32[2,256,256]{2,1,0:T(8,128)}, u32[]{:S(2)}, u32[]{:S(2)}) collective-permute-start(f32[2,256,256]{2,1,0:T(8,128)} %get-tuple-element.20), channel_id=1, source_target_pairs={{0,1},{1,2},{2,3},{3,4},{4,5},{5,6},{6,7},{8,9},{9,10},{10,11},{11... | collective-permute-start | bytes 1572872 | tf_op jit(solution)/shard_map/ppermute | solution.py:21
  69.5 1.4 %collective-permute-start.12 = (f32[2,256,512]{2,1,0:T(8,128)}, f32[2,256,512]{2,1,0:T(8,128)S(1)}, u32[]{:S(2)}, u32[]{:S(2)}) collective-permute-start(f32[2,256,512]{2,1,0:T(8,128)} %get-tuple-element.23), channel_id=1, source_target_pairs={{0,8},{8,16},{16,24},{1,9},{9,17},{17,25},{2,10},{10,18},{18,26},{... | collective-permute-start | bytes 3145736 | tf_op jit(solution)/shard_map/ppermute | solution.py:21
  71.0 0.9 dynamic-slice_add_fusion.1
  71.9 3.1 %collective-permute-start.7 = (f32[64,256]{1,0:T(8,128)S(1)}, f32[64,256]{1,0:T(8,128)S(1)}, u32[]{:S(2)}, u32[]{:S(2)}) collective-permute-start(f32[64,256]{1,0:T(8,128)S(1)} %constant_dynamic-slice_fusion), channel_id=1, source_target_pairs={{0,1},{1,0},{2,3},{3,2},{4,5},{5,4},{6,7},{7,6},{8,9},{9,8},{10,11... | collective-permute-start | bytes 196616 | tf_op jit(solution)/shard_map/ppermute | solution.py:30
  75.1 11.6 %collective-permute-done.7 = f32[64,256]{1,0:T(8,128)S(1)} collective-permute-done((f32[64,256]{1,0:T(8,128)S(1)}, f32[64,256]{1,0:T(8,128)S(1)}, u32[]{:S(2)}, u32[]{:S(2)}) %collective-permute-start.7) | collective-permute-done | bytes 65568 | tf_op jit(solution)/shard_map/ppermute | solution.py:30
  86.7 0.7 collective-permute-start.8
  87.4 2.1 %add.65 = f32[2,256,256]{2,1,0:T(8,128)} add(f32[2,256,256]{2,1,0:T(8,128)} %get-tuple-element.24, f32[2,256,256]{2,1,0:T(8,128)} %copy-done.2) | non-fusion elementwise | flops 131072 | bytes 1572864 | tf_op jit(solution)/shard_map/add | solution.py:238
  89.5 1.3 %collective-permute-start.13 = (f32[2,256,256]{2,1,0:T(8,128)}, f32[2,256,256]{2,1,0:T(8,128)}, u32[]{:S(2)}, u32[]{:S(2)}) collective-permute-start(f32[2,256,256]{2,1,0:T(8,128)} %add.65), channel_id=1, source_target_pairs={{0,1},{1,2},{2,3},{3,4},{4,5},{5,6},{6,7},{8,9},{9,10},{10,11},{11... | collective-permute-start | bytes 1572872 | tf_op jit(solution)/shard_map/ppermute | solution.py:21
  90.8 4.6 %collective-permute-start.10 = (f32[64,256]{1,0:T(8,128)S(1)}, f32[64,256]{1,0:T(8,128)S(1)}, u32[]{:S(2)}, u32[]{:S(2)}) collective-permute-start(f32[64,256]{1,0:T(8,128)S(1)} %add.63), channel_id=1, source_target_pairs={{0,4},{1,5},{2,6},{3,7},{4,0},{5,1},{6,2},{7,3},{8,12},{9,13},{10,... | collective-permute-start | bytes 196616 | tf_op jit(solution)/shard_map/ppermute | solution.py:30
  95.4 13.8 %collective-permute-done.10 = f32[64,256]{1,0:T(8,128)S(1)} collective-permute-done((f32[64,256]{1,0:T(8,128)S(1)}, f32[64,256]{1,0:T(8,128)S(1)}, u32[]{:S(2)}, u32[]{:S(2)}) %collective-permute-start.10) | collective-permute-done | bytes 65568 | tf_op jit(solution)/shard_map/ppermute | solution.py:30
  109.3 3.1 %collective-permute-done.11 = f32[64,256]{1,0:T(8,128)S(1)} collective-permute-done((f32[64,256]{1,0:T(8,128)S(1)}, f32[64,256]{1,0:T(8,128)S(1)}, u32[]{:S(2)}, u32[]{:S(2)}) %collective-permute-start.11) | collective-permute-done | bytes 65568 | tf_op jit(solution)/shard_map/ppermute | solution.py:30
  112.5 0.3 collective-permute-start.14
  112.7 3.6 %collective-permute-done.14 = f32[128,256]{1,0:T(8,128)S(1)} collective-permute-done((f32[128,256]{1,0:T(8,128)S(1)}, f32[128,256]{1,0:T(8,128)S(1)}, u32[]{:S(2)}, u32[]{:S(2)}) %collective-permute-start.14) | collective-permute-done | bytes 131104 | tf_op jit(solution)/shard_map/ppermute | solution.py:30
  116.4 4.3 %collective-permute-start.15 = (f32[256,256]{1,0:T(8,128)S(1)}, f32[256,256]{1,0:T(8,128)S(1)}, u32[]{:S(2)}, u32[]{:S(2)}) collective-permute-start(f32[256,256]{1,0:T(8,128)S(1)} %pad_maximum_fusion), channel_id=1, source_target_pairs={{0,8},{8,0},{16,24},{24,16},{1,9},{9,1},{17,25},{25,17},{2,10},{10... | collective-permute-start | bytes 786440 | tf_op jit(solution)/shard_map/ppermute | solution.py:30
  120.7 2.9 %pad_add_fusion = f32[2,512,512]{2,1,0:T(8,128)} fusion(f32[2,256,256]{2,1,0:T(8,128)} %collective-permute-done.9, f32[2,256,256]{2,1,0:T(8,128)} %collective-permute-done.13, f32[2,512,512]{2,1,0:T(8,128)S(1)} %copy-done, f32[2,256,512]{2,1,0:T(8,128)S(1)} %collective-permute-done.12), kind=kLoop, calls=%fused_computation | loop fusion | flops 1572864 | bytes 6291456 | tf_op jit(solution)/shard_map/add | solution.py:246
  123.7 0.8 maximum_multiply_fusion
  (32 shorter events, 0.4 us)
Async XLA Ops:
  0.6 4.1 %copy-start.1 = (f32[2,512,512]{2,1,0:T(8,128)S(1)}, f32[2,512,512]{2,1,0:T(8,128)}, u32[]{:S(2)}) copy-start(f32[2,512,512]{2,1,0:T(8,128)} %obj.1) | copy-start | bytes 6291460
  0.6 21.5 %copy-start.3 = (s32[1,1,8,2]{2,3,1,0:T(2,128)S(1)}, s32[1,1,8,2]{2,3,1,0:T(2,128)}, u32[]{:S(2)}) copy-start(s32[1,1,8,2]{2,3,1,0:T(2,128)} %param.9) | copy-start | bytes 196
  2.1 27.6 %collective-permute-start = (f32[2,256,512]{2,1,0:T(8,128)S(1)}, f32[2,256,512]{2,1,0:T(8,128)S(1)}, u32[]{:S(2)}, u32[]{:S(2)}) collective-permute-start(f32[2,256,512]{2,1,0:T(8,128)S(1)} %slice.9), channel_id=1, source_target_pairs={{8,0},{16,8},{24,16},{9,1},{17,9},{25,17},{10,2},{18,10},{26,18},{... | collective-permute-start | bytes 3145736 | tf_op jit(solution)/shard_map/ppermute | solution.py:21
  4.9 13.5 %collective-permute-start.1 = (f32[2,256,256]{2,1,0:T(8,128)S(1)}, f32[2,256,256]{2,1,0:T(8,128)S(1)}, u32[]{:S(2)}, u32[]{:S(2)}) collective-permute-start(f32[2,256,256]{2,1,0:T(8,128)S(1)} %get-tuple-element.31), channel_id=1, source_target_pairs={{1,0},{2,1},{3,2},{4,3},{5,4},{6,5},{7,6},{9,8},{10,9},{11,10},{12... | collective-permute-start | bytes 1572872 | tf_op jit(solution)/shard_map/ppermute | solution.py:21
  7.0 22.6 %collective-permute-start.2 = (f32[2,256,256]{2,1,0:T(8,128)S(1)}, f32[2,256,256]{2,1,0:T(8,128)}, u32[]{:S(2)}, u32[]{:S(2)}) collective-permute-start(f32[2,256,256]{2,1,0:T(8,128)S(1)} %get-tuple-element.30), channel_id=1, source_target_pairs={{1,0},{2,1},{3,2},{4,3},{5,4},{6,5},{7,6},{9,8},{10,9},{11,10},{12... | collective-permute-start | bytes 1572872 | tf_op jit(solution)/shard_map/ppermute | solution.py:21
  18.4 11.2 %copy-start.5 = (f32[2,256,256]{2,1,0:T(8,128)}, f32[2,256,256]{2,1,0:T(8,128)S(1)}, u32[]{:S(2)}) copy-start(f32[2,256,256]{2,1,0:T(8,128)S(1)} %collective-permute-done.1.right_top) | copy-start | bytes 1572868
  18.4 11.2 %collective-permute-start.3 = (f32[2,256,256]{2,1,0:T(8,128)S(1)}, f32[2,256,256]{2,1,0:T(8,128)}, u32[]{:S(2)}, u32[]{:S(2)}) collective-permute-start(f32[2,256,256]{2,1,0:T(8,128)S(1)} %collective-permute-done.1.right_top), channel_id=1, source_target_pairs={{8,0},{16,8},{24,16},{9,1},{17,9},{25,17},{10,2},{18,10},{26,18},{... | collective-permute-start | bytes 1572872 | tf_op jit(solution)/shard_map/ppermute | solution.py:21
  29.7 1.0 copy-start.4
  57.8 5.8 %collective-permute-start.5 = (f32[2,256,256]{2,1,0:T(8,128)}, f32[2,256,256]{2,1,0:T(8,128)S(1)}, u32[]{:S(2)}, u32[]{:S(2)}) collective-permute-start(f32[2,256,256]{2,1,0:T(8,128)} %get-tuple-element.18), channel_id=1, source_target_pairs={{0,8},{8,16},{16,24},{1,9},{9,17},{17,25},{2,10},{10,18},{18,26},{... | collective-permute-start | bytes 1572872 | tf_op jit(solution)/shard_map/ppermute | solution.py:21
  60.1 2.5 %collective-permute-start.4 = (f32[256,256]{1,0:T(8,128)S(1)}, f32[256,256]{1,0:T(8,128)S(1)}, u32[]{:S(2)}, u32[]{:S(2)}) collective-permute-start(f32[256,256]{1,0:T(8,128)S(1)} %constant_dynamic-slice_fusion.2), channel_id=1, source_target_pairs={{0,8},{8,0},{16,24},{24,16},{1,9},{9,1},{17,25},{25,17},{2,10},{10... | collective-permute-start | bytes 786440 | tf_op jit(solution)/shard_map/ppermute | solution.py:30
  63.6 5.9 %copy-start.2 = (f32[2,256,256]{2,1,0:T(8,128)}, f32[2,256,256]{2,1,0:T(8,128)S(1)}, u32[]{:S(2)}) copy-start(f32[2,256,256]{2,1,0:T(8,128)S(1)} %collective-permute-done.5) | copy-start | bytes 1572868
  63.6 7.3 %collective-permute-start.6 = (f32[128,256]{1,0:T(8,128)S(1)}, f32[128,256]{1,0:T(8,128)}, u32[]{:S(2)}, u32[]{:S(2)}) collective-permute-start(f32[128,256]{1,0:T(8,128)S(1)} %constant_dynamic-slice_fusion.1), channel_id=1, source_target_pairs={{0,16},{8,24},{16,0},{24,8},{1,17},{9,25},{17,1},{25,9},{2,18},{10... | collective-permute-start | bytes 393224 | tf_op jit(solution)/shard_map/ppermute | solution.py:30
  68.2 22.6 %collective-permute-start.9 = (f32[2,256,256]{2,1,0:T(8,128)}, f32[2,256,256]{2,1,0:T(8,128)}, u32[]{:S(2)}, u32[]{:S(2)}) collective-permute-start(f32[2,256,256]{2,1,0:T(8,128)} %get-tuple-element.20), channel_id=1, source_target_pairs={{0,1},{1,2},{2,3},{3,4},{4,5},{5,6},{6,7},{8,9},{9,10},{10,11},{11... | collective-permute-start | bytes 1572872 | tf_op jit(solution)/shard_map/ppermute | solution.py:21
  69.5 51.2 %copy-start = (f32[2,512,512]{2,1,0:T(8,128)S(1)}, f32[2,512,512]{2,1,0:T(8,128)}, u32[]{:S(2)}) copy-start(f32[2,512,512]{2,1,0:T(8,128)} %get-tuple-element.16) | copy-start | bytes 6291460
  69.5 42.9 %collective-permute-start.12 = (f32[2,256,512]{2,1,0:T(8,128)}, f32[2,256,512]{2,1,0:T(8,128)S(1)}, u32[]{:S(2)}, u32[]{:S(2)}) collective-permute-start(f32[2,256,512]{2,1,0:T(8,128)} %get-tuple-element.23), channel_id=1, source_target_pairs={{0,8},{8,16},{16,24},{1,9},{9,17},{17,25},{2,10},{10,18},{18,26},{... | collective-permute-start | bytes 3145736 | tf_op jit(solution)/shard_map/ppermute | solution.py:21
  71.9 14.8 %collective-permute-start.7 = (f32[64,256]{1,0:T(8,128)S(1)}, f32[64,256]{1,0:T(8,128)S(1)}, u32[]{:S(2)}, u32[]{:S(2)}) collective-permute-start(f32[64,256]{1,0:T(8,128)S(1)} %constant_dynamic-slice_fusion), channel_id=1, source_target_pairs={{0,1},{1,0},{2,3},{3,2},{4,5},{5,4},{6,7},{7,6},{8,9},{9,8},{10,11... | collective-permute-start | bytes 196616 | tf_op jit(solution)/shard_map/ppermute | solution.py:30
  86.7 4.1 %collective-permute-start.8 = (f32[64,256]{1,0:T(8,128)S(1)}, f32[64,256]{1,0:T(8,128)S(1)}, u32[]{:S(2)}, u32[]{:S(2)}) collective-permute-start(f32[64,256]{1,0:T(8,128)S(1)} %dynamic-slice_add_fusion.2), channel_id=1, source_target_pairs={{0,2},{1,3},{2,0},{3,1},{4,6},{5,7},{6,4},{7,5},{8,10},{9,11},{10,... | collective-permute-start | bytes 196616 | tf_op jit(solution)/shard_map/ppermute | solution.py:30
  89.5 23.0 %collective-permute-start.13 = (f32[2,256,256]{2,1,0:T(8,128)}, f32[2,256,256]{2,1,0:T(8,128)}, u32[]{:S(2)}, u32[]{:S(2)}) collective-permute-start(f32[2,256,256]{2,1,0:T(8,128)} %add.65), channel_id=1, source_target_pairs={{0,1},{1,2},{2,3},{3,4},{4,5},{5,6},{6,7},{8,9},{9,10},{10,11},{11... | collective-permute-start | bytes 1572872 | tf_op jit(solution)/shard_map/ppermute | solution.py:21
  90.8 18.4 %collective-permute-start.10 = (f32[64,256]{1,0:T(8,128)S(1)}, f32[64,256]{1,0:T(8,128)S(1)}, u32[]{:S(2)}, u32[]{:S(2)}) collective-permute-start(f32[64,256]{1,0:T(8,128)S(1)} %add.63), channel_id=1, source_target_pairs={{0,4},{1,5},{2,6},{3,7},{4,0},{5,1},{6,2},{7,3},{8,12},{9,13},{10,... | collective-permute-start | bytes 196616 | tf_op jit(solution)/shard_map/ppermute | solution.py:30
  109.2 3.2 %collective-permute-start.11 = (f32[64,256]{1,0:T(8,128)S(1)}, f32[64,256]{1,0:T(8,128)S(1)}, u32[]{:S(2)}, u32[]{:S(2)}) collective-permute-start(f32[64,256]{1,0:T(8,128)S(1)} %add.64), channel_id=1, source_target_pairs={{0,1},{1,0},{2,3},{3,2},{4,5},{5,4},{6,7},{7,6},{8,9},{9,8},{10,11... | collective-permute-start | bytes 196616 | tf_op jit(solution)/shard_map/ppermute | solution.py:30
  112.5 3.9 %collective-permute-start.14 = (f32[128,256]{1,0:T(8,128)S(1)}, f32[128,256]{1,0:T(8,128)S(1)}, u32[]{:S(2)}, u32[]{:S(2)}) collective-permute-start(f32[128,256]{1,0:T(8,128)S(1)} %pad_maximum_fusion.1), channel_id=1, source_target_pairs={{0,16},{8,24},{16,0},{24,8},{1,17},{9,25},{17,1},{25,9},{2,18},{10... | collective-permute-start | bytes 393224 | tf_op jit(solution)/shard_map/ppermute | solution.py:30
  116.4 7.3 %collective-permute-start.15 = (f32[256,256]{1,0:T(8,128)S(1)}, f32[256,256]{1,0:T(8,128)S(1)}, u32[]{:S(2)}, u32[]{:S(2)}) collective-permute-start(f32[256,256]{1,0:T(8,128)S(1)} %pad_maximum_fusion), channel_id=1, source_target_pairs={{0,8},{8,0},{16,24},{24,16},{1,9},{9,1},{17,25},{25,17},{2,10},{10... | collective-permute-start | bytes 786440 | tf_op jit(solution)/shard_map/ppermute | solution.py:30
